TPU v7x, 1024 devices: a whole 4x4x32 slice. The times are simulated.
1024 devices in a mesh: row: 8 (over x, core), col: 128 (over y, z).
Axes of the slice: x: 4, y: 4, z: 32, core: 2. Of those that a mesh axis runs over, the one named last changes fastest.
Arguments:
- tokens: bfloat16 [2048, 8192], P('col', 'row'), may hold values from -6 to 6
- route_index: int32 [512], replicated, may hold values from 0 to 2047, as said below
- router_score: float32 [512], replicated, may hold values from 0.1 to 1
- out_grad: bfloat16 [512, 8192], P(None, 'row'), may hold values from -6 to 6
- gate_weight: bfloat16 [8192, 22016], P('row', 'col'), may hold values from -0.0625 to 0.0625
- up_weight: bfloat16 [8192, 22016], P('row', 'col'), may hold values from -0.0625 to 0.0625
- down_weight: bfloat16 [22016, 8192], P('col', 'row'), may hold values from -0.0390625 to 0.0390625
Outputs:
- d_rows: bfloat16 [512, 8192], P('col', 'row')
- d_gate: bfloat16 [8192, 22016], P('row', 'col')
- d_up: bfloat16 [8192, 22016], P('row', 'col')
- d_down: bfloat16 [22016, 8192], P('col', 'row')
Inputs may be any that keep to these rules, and one draw needn't show every extreme that they name: `route_index`: the 512 entries are distinct tokens of the micro-batch; the last token is always among them.
All inputs are finite; a program needn't handle non-finite values.
Results may differ from a plain program's by a relative error of at most 0.0057.
Values may be sent and summed in bfloat16 or wider, within the bound.
No kernel may reach another device: no remote copies, remote signals or barrier semaphores. Data moves between devices by JAX's collectives and lax.ppermute only.
A program may use at most 32 MiB of HBM per device.

v0:
```python
import jax
import jax.numpy as jnp
from jax import lax
from jax.sharding import PartitionSpec as P


def activate(gate, up, back):
    sig = jax.nn.sigmoid(gate)
    silu = gate * sig
    hidden = (silu * up).astype(jnp.bfloat16)
    grad_up = (back * silu).astype(jnp.bfloat16)
    grad_gate = (back * up * sig * (1.0 + gate * (1.0 - sig))).astype(jnp.bfloat16)
    return (hidden, grad_up, grad_gate)


def body(tokens, route_index, router_score, out_grad, gate_weight, up_weight, down_weight):
    count_rows = route_index.shape[0]
    width_here = tokens.shape[1]
    empty = jnp.zeros((count_rows, width_here), jnp.bfloat16)
    piece = lax.all_gather(tokens, "col", axis=0, tiled=True)
    inside = (route_index >= 0) & (route_index < piece.shape[0])
    rows_found = jnp.take(piece, jnp.clip(route_index, 0, piece.shape[0] - 1), axis=0)
    routed = jnp.where(inside[:, None], rows_found, empty)
    scaled = (router_score[:, None] * out_grad.astype(jnp.float32)).astype(jnp.bfloat16)
    gate_part = jnp.dot(routed, gate_weight, preferred_element_type=jnp.float32)
    up_part = jnp.dot(routed, up_weight, preferred_element_type=jnp.float32)
    back_part = lax.dot_general(
        scaled, down_weight, (((1,), (1,)), ((), ())), preferred_element_type=jnp.float32
    )
    gate, up, back = lax.psum((gate_part, up_part, back_part), "row")
    hidden, grad_up, grad_gate = activate(gate, up, back)
    d_down = lax.dot_general(
        hidden, scaled, (((0,), (0,)), ((), ())), preferred_element_type=jnp.float32
    ).astype(jnp.bfloat16)
    d_gate = lax.dot_general(
        routed, grad_gate, (((0,), (0,)), ((), ())), preferred_element_type=jnp.float32
    ).astype(jnp.bfloat16)
    d_up = lax.dot_general(
        routed, grad_up, (((0,), (0,)), ((), ())), preferred_element_type=jnp.float32
    ).astype(jnp.bfloat16)
    own_rows = count_rows // lax.axis_size("col")
    total = lax.dot_general(
        grad_gate, gate_weight, (((1,), (1,)), ((), ())), preferred_element_type=jnp.float32
    )
    summed = lax.psum_scatter(
        total
        + lax.dot_general(
            grad_up, up_weight, (((1,), (1,)), ((), ())), preferred_element_type=jnp.float32
        ),
        "col",
        scatter_dimension=0,
        tiled=True,
    )
    mine = lax.dynamic_slice_in_dim(out_grad, lax.axis_index("col") * own_rows, own_rows, 0)
    d_rows = (mine.astype(jnp.float32) + summed).astype(jnp.bfloat16)
    return (d_rows, d_gate, d_up, d_down)


def solution(mesh):
    placed = (
        P("col", "row"),
        P(),
        P(),
        P(None, "row"),
        P("row", "col"),
        P("row", "col"),
        P("col", "row"),
    )
    return jax.shard_map(
        body,
        mesh=mesh,
        in_specs=placed,
        out_specs=(P("col", "row"), P("row", "col"), P("row", "col"), P("col", "row")),
        check_vma=False,
    )
```

profile of v0, /device:TPU:2, one launch (start us, length us, event | category | flops | bytes accessed | tf_op | source)
XLA Modules:
  0.0 920.2 jit_solution(17278562857468738727)
XLA Ops:
  7.2 0.0 copy-start
  7.2 0.0 all-gather.2.cloned.1.call-start
  7.2 0.7 all-gather.2.cloned.1.call-update
  7.9 0.0 all-reduce.7.cloned.1.call-start
  8.0 0.7 compare_select_fusion
  8.7 0.7 compare_and_fusion.1
  9.4 2.6 fusion
  12.0 281.0 %all-gather.2.cloned.1.call-done = bf16[2048,1024]{1,0:T(8,128)(2,1)} async-done(((bf16[16,1024]{1,0:T(8,128)(2,1)}), bf16[2048,1024]{1,0:T(8,128)(2,1)}) %all-gather.2.cloned.1.call-update) | async-done | bytes 4194320 | tf_op jit(solution)/shard_map/all_gather | solution.py:20
  293.0 5.5 gather_fusion
  298.4 0.0 copy-start.1
  298.4 0.2 select_select_fusion
  298.7 0.0 copy-done
  298.7 1.2 fusion.6
  299.9 0.0 copy-done.1
  299.9 1.2 fusion.5
  301.2 0.0 all-reduce.7.cloned.1.call-update
  301.2 0.0 all-reduce.5.cloned.1.call-start
  301.2 86.7 %all-reduce.7.cloned.1.call-done = (f32[512,172]{0,1:T(8,128)}, f32[512,172]{0,1:T(8,128)}, f32[512,172]{0,1:T(8,128)}) async-done(((f32[512,172]{0,1:T(8,128)}, f32[512,172]{0,1:T(8,128)}, f32[512,172]{0,1:T(8,128)}), (f32[512,172]{0,1:T(8,128)}, f32[512,172]{0,1:T(8,128)}, f32[512,172]{0,1:T(8,128)})) %all-reduce.7.cloned.1.call-update) | async-done | bytes 1056784 | tf_op jit(solution)/shard_map/psum | solution.py:30
  387.9 1.4 multiply_convert_fusion.4
  389.3 0.5 fusion.7
  389.8 1.8 convolution_add_fusion
  391.5 0.0 all-reduce.5.cloned.1.call-update
  391.6 0.0 copy-start.2
  391.6 0.0 copy-start.3
  391.6 0.0 copy-start.4
  391.6 0.0 copy-start.5
  391.6 1.4 dynamic-slice
  393.7 1.1 convolution_convert_fusion.1
  394.8 1.1 convolution_convert_fusion.2
  395.9 0.0 copy-done.2
  395.9 0.0 copy-done.3
  395.9 0.0 copy-done.4
  395.9 0.0 copy-done.5
  395.9 1.3 convolution_convert_fusion
  397.1 515.2 %all-reduce.5.cloned.1.call-done = f32[512,1024]{1,0:T(8,128)} async-done(((f32[512,1024]{1,0:T(8,128)}), f32[512,1024]{1,0:T(8,128)}) %all-reduce.5.cloned.1.call-update) | async-done | bytes 2097168
  912.3 1.4 fusion.3
  (1 shorter events, 0.0 us)
Async XLA Ops:
  7.2 291.5 %copy-start = (bf16[1024,172]{0,1:T(8,128)(2,1)S(1)}, bf16[1024,172]{0,1:T(8,128)(2,1)}, u32[]{:S(2)}) copy-start(bf16[1024,172]{0,1:T(8,128)(2,1)} %param.11) | copy-start | bytes 1056772
  7.2 285.8 %all-gather.2.cloned.1.call-start = ((), (), s32[]{:S(2)}) async-start(), calls=%async_computation | async-start | bytes 4227072 | tf_op jit(solution)/shard_map/all_gather | solution.py:20
  7.9 380.0 %all-reduce.7.cloned.1.call-start = ((), (), s32[]{:S(2)}) async-start(), calls=%async_computation.2 | async-start | bytes 2162688 | tf_op jit(solution)/shard_map/psum | solution.py:30
  298.4 1.5 copy-start.1
  301.2 611.1 %all-reduce.5.cloned.1.call-start = ((), (), s32[]{:S(2)}) async-start(), calls=%async_computation.1 | async-start | bytes 4194304
  391.6 4.3 copy-start.2
  391.6 4.3 copy-start.3
  391.6 4.3 copy-start.4
  391.6 4.3 copy-start.5
Sparse Core Ops, SparseCore 0:
  12.1 280.8 all-gather.1
  301.3 86.5 all-reduce.6
  391.7 520.5 all-reduce.4
where the time goes:
time: 921 us; the launch traced here: 920 us
  waiting for transfers between devices  884 us (96%)
  between operations  14.5 us (2%)
  matrix products  10.8 us (1%)
    unnamed x4, waiting for transfers between devices  516 us
    all_gather x1, waiting for transfers between devices, body(): piece = lax.all_gather(tokens, 'col', axis=0, tiled=True)  281 us
    psum x1, waiting for transfers between devices, body(): gate, up, back = lax.psum((gate_part, up_part, back_part), 'row')  86.7 us
  transfers between devices with their start and end apart: 3, of which 3 were waited for; matrix products, arithmetic and copies ran while one was open for 1% of the time, Pallas kernels for 0%

commit v1 on v0

v1 whole, which is shorter than its diff:
```python
import jax
import jax.numpy as jnp
from jax import lax
from jax.sharding import Mesh
from jax.sharding import PartitionSpec as P

BF = jnp.bfloat16
F32 = jnp.float32


def exchange(x, axis):
    return lax.all_to_all(x, axis, 0, 0, tiled=True)


def to_all(x, axis, count):
    return exchange(jnp.broadcast_to(x[None], (count,) + x.shape), axis)


def gather_routed(tokens, route_index):
    here, width = tokens.shape
    ny, nh, nl = lax.axis_size("y"), lax.axis_size("zh"), lax.axis_size("zl")
    quarter = width // nl
    rows = route_index.shape[0]
    cut = tokens.reshape(here, nl, quarter).transpose(1, 0, 2)
    cut = jnp.broadcast_to(cut[None], (ny, nl, here, quarter)).reshape(ny * nl, here, quarter)
    held = exchange(cut, ("y", "zl")).reshape(ny * nl * here, quarter)
    slots = rows // ny
    mine = lax.dynamic_slice_in_dim(route_index, lax.axis_index("y") * slots, slots, 0)
    owner, inner = mine // here, mine % here
    y, zh, zl = owner // (nh * nl), (owner // nl) % nh, owner % nl
    place = jnp.where(zh == lax.axis_index("zh"), (y * nl + zl) * here + inner, -1)
    pick = (place[:, None] == lax.broadcasted_iota(jnp.int32, (slots, ny * nl * here), 1)).astype(BF)
    filled = jnp.dot(pick, held, preferred_element_type=F32).astype(BF)
    each = slots // (nh * nl)
    got = exchange(filled.reshape(nh * nl, each, quarter), ("zh", "zl"))
    got = got.reshape(nh, nl, each, quarter).astype(F32).sum(0).astype(BF)
    got = jnp.broadcast_to(got[None], (nh, nl, each, quarter)).reshape(nh * nl, each, quarter)
    got = exchange(got, ("zh", "zl")).reshape(slots, quarter)
    got = to_all(got, "zl", nl).transpose(1, 0, 2).reshape(slots, width)
    return to_all(got, "y", ny).reshape(rows, width)


def activate(gate, up, back):
    sig = jax.nn.sigmoid(gate)
    silu = gate * sig
    hidden = (silu * up).astype(BF)
    grad_up = (back * silu).astype(BF)
    grad_gate = (back * up * sig * (1.0 + gate * (1.0 - sig))).astype(BF)
    return (hidden, grad_up, grad_gate)


def sum_and_activate(parts):
    nx, nc = lax.axis_size("x"), lax.axis_size("core")
    half = parts.shape[2] // nc
    core = lax.axis_index("core")
    keep = lax.dynamic_slice_in_dim(parts, core * half, half, 2)
    give = lax.dynamic_slice_in_dim(parts, (1 - core) * half, half, 2)
    chip = (keep + lax.ppermute(give, "core", [(0, 1), (1, 0)])).astype(BF)
    gate, up, back = to_all(chip, "x", nx).astype(F32).sum(0)
    out = jnp.stack(activate(gate, up, back))
    return lax.all_gather(out, "core", axis=2, tiled=True)


def scatter_rows(total, out_grad):
    rows, width = total.shape
    ny, nh, nl = lax.axis_size("y"), lax.axis_size("zh"), lax.axis_size("zl")
    slots, quarter = rows // ny, width // nl
    each = slots // (nh * nl)
    part = exchange(total.reshape(ny, slots, width), "y").astype(F32).sum(0).astype(BF)
    part = part.reshape(slots, nl, quarter).transpose(1, 0, 2)
    part = exchange(part, "zl").astype(F32).sum(0).astype(BF)
    part = exchange(part.reshape(nh * nl, each, quarter), ("zh", "zl"))
    part = part.reshape(nh, nl, each, quarter).astype(F32).sum(0)
    part = part.transpose(1, 0, 2).reshape(each, width)
    first = lax.axis_index(("y", "zh", "zl")) * each
    mine = lax.dynamic_slice_in_dim(out_grad, first, each, 0)
    return (mine.astype(F32) + part).astype(BF)


def body(tokens, route_index, router_score, out_grad, gate_weight, up_weight, down_weight):
    routed = gather_routed(tokens, route_index)
    scaled = (router_score[:, None] * out_grad.astype(F32)).astype(BF)
    dot = lambda a, b, i, j: lax.dot_general(a, b, (((i,), (j,)), ((), ())), preferred_element_type=F32)
    parts = jnp.stack(
        [
            dot(gate_weight, routed, 0, 1),
            dot(up_weight, routed, 0, 1),
            dot(down_weight, scaled, 1, 1),
        ]
    )
    hidden, grad_up, grad_gate = sum_and_activate(parts)
    d_down = dot(hidden, scaled, 1, 0).astype(BF)
    d_gate = dot(routed, grad_gate, 0, 1).astype(BF)
    d_up = dot(routed, grad_up, 0, 1).astype(BF)
    total = dot(grad_gate, gate_weight, 0, 1) + dot(grad_up, up_weight, 0, 1)
    d_rows = scatter_rows(total.astype(BF), out_grad)
    return (d_rows, d_gate, d_up, d_down)


def solution(mesh):
    rows, cols = mesh.devices.shape
    fine = Mesh(mesh.devices.reshape(rows // 2, 2, 4, cols // 16, 4), ("x", "core", "y", "zh", "zl"))
    row, col = ("x", "core"), ("y", "zh", "zl")
    placed = (
        P(col, row),
        P(),
        P(),
        P(None, row),
        P(row, col),
        P(row, col),
        P(col, row),
    )
    return jax.shard_map(
        body,
        mesh=fine,
        in_specs=placed,
        out_specs=(P(col, row), P(row, col), P(row, col), P(col, row)),
        check_vma=False,
    )
```

time: 921 us -> 215 us (0.23)
  waiting for transfers between devices: 884 us -> 47.9 us
  blocking collectives: 0 us -> 127 us
  starting transfers between devices: 0.12 us -> 21.8 us
  between operations: 14.5 us -> 0.87 us
    unnamed x4 -> x0, waiting for transfers between devices: 516 us -> none
    all_gather x1 -> x0, waiting for transfers between devices: 281 us -> none  [body(): piece = lax.all_gather(tokens, 'col', axis=0, tiled=True)]
    all_to_all x0 -> x5, blocking collectives: none -> 124 us  [exchange(): return lax.all_to_all(x, axis, 0, 0, tiled=True)]
    psum x1 -> x0, waiting for transfers between devices: 86.7 us -> none  [body(): gate, up, back = lax.psum((gate_part, up_part, back_part), 'row')]
    all_to_all x0 -> x4, waiting for transfers between devices: none -> 45.7 us  [exchange(): return lax.all_to_all(x, axis, 0, 0, tiled=True)]
    all_to_all x0 -> x4, starting transfers between devices: none -> 19.8 us  [exchange(): return lax.all_to_all(x, axis, 0, 0, tiled=True)]
  transfers between devices with their start and end apart: 3 -> 5, of which waited for: 3 -> 5; matrix products, arithmetic and copies ran while one was open for 1% -> 3% of each run, Pallas kernels for 0% -> 0%
where the time goes in v1:
time: 215 us
  blocking collectives  127 us (59%)
  waiting for transfers between devices  47.9 us (22%)
  starting transfers between devices  21.8 us (10%)
  matrix products  8.05 us (4%)
  local copies, waits for them, and re-layouts  5.57 us (3%)
  other arithmetic  3.92 us (2%)
    all_to_all x5, blocking collectives, exchange(): return lax.all_to_all(x, axis, 0, 0, tiled=True)  124 us
    all_to_all x4, waiting for transfers between devices, exchange(): return lax.all_to_all(x, axis, 0, 0, tiled=True)  45.7 us
    all_to_all x4, starting transfers between devices, exchange(): return lax.all_to_all(x, axis, 0, 0, tiled=True)  19.8 us
    dot_general x8, matrix products, body(): lax.dot_general(a, b, (((i,), (j,)), ((), ())), preferred_element_type=F32)  7.84 us
  transfers between devices with their start and end apart: 5, of which 5 were waited for; matrix products, arithmetic and copies ran while one was open for 3% of the time, Pallas kernels for 0%

profile of v1, /device:TPU:2, one launch (start us, length us, event | category | flops | bytes accessed | tf_op | source)
XLA Modules:
  0.0 214.6 jit_solution(2287906885781064764)
XLA Ops:
  0.6 0.0 copy-start
  0.6 0.8 reshape.51
  1.5 0.7 broadcast_in_dim.16
  2.2 8.6 %all-to-all-start = ((bf16[16,16,256]{2,1,0:T(8,128)(2,1)}), bf16[16,16,256]{2,1,0:T(8,128)(2,1)S(1)}, u32[]{:S(2)}, u32[]{:S(2)}) async-start(bf16[16,16,256]{2,1,0:T(8,128)(2,1)} %bitcast.1), calls=%async_computation | async-start | bytes 262144 | tf_op jit(solution)/shard_map/all_to_all | solution.py:12
  10.8 0.8 compare_select_fusion.2
  11.6 7.6 %all-to-all-done = bf16[16,16,256]{2,1,0:T(8,128)(2,1)S(1)} async-done(((bf16[16,16,256]{2,1,0:T(8,128)(2,1)}), bf16[16,16,256]{2,1,0:T(8,128)(2,1)S(1)}, u32[]{:S(2)}, u32[]{:S(2)}) %all-to-all-start) | async-done | bytes 131104 | tf_op jit(solution)/shard_map/all_to_all | solution.py:12
  19.2 0.2 convolution_convert_fusion.3
  19.4 50.3 %all_to_all.45 = bf16[32,4,256]{2,1,0:T(4,128)(2,1)S(1)} all-to-all(bf16[32,4,256]{2,1,0:T(4,128)(2,1)S(1)} %reshape.54), channel_id=1, replica_groups=mesh['x'=4,'core'=2,'y'=4,'zh'=8,'zl'=4] {'zh','zl'}, dimensions={0} | all-to-all | bytes 131072 | tf_op jit(solution)/shard_map/all_to_all | solution.py:12
  69.9 27.5 %all_to_all.46 = bf16[32,4,256]{2,1,0:T(4,128)(2,1)S(1)} all-to-all(bf16[32,4,256]{2,1,0:T(4,128)(2,1)S(1)} %bitcast.61), channel_id=1, replica_groups=mesh['x'=4,'core'=2,'y'=4,'zh'=8,'zl'=4] {'zh','zl'}, dimensions={0} | all-to-all | bytes 131072 | tf_op jit(solution)/shard_map/all_to_all | solution.py:12
  97.4 0.1 copy.41
  97.5 9.5 %all_to_all.47 = bf16[4,128,256]{1,2,0:T(8,128)(2,1)S(1)} all-to-all(bf16[4,128,256]{1,2,0:T(8,128)(2,1)S(1)} %broadcast_in_dim.19), channel_id=1, replica_groups=mesh['x'=4,'core'=2,'y'=4,'zh'=8,'zl'=4] {'zl'}, dimensions={0} | all-to-all | bytes 524288 | tf_op jit(solution)/shard_map/all_to_all | solution.py:12
  107.0 0.1 copy.42
  107.2 1.1 broadcast_in_dim.21
  108.3 3.6 %all-to-all-start.4 = ((bf16[4,128,1024]{2,1,0:T(8,128)(2,1)}), bf16[4,128,1024]{2,1,0:T(8,128)(2,1)S(1)}, u32[]{:S(2)}, u32[]{:S(2)}) async-start(bf16[4,128,1024]{2,1,0:T(8,128)(2,1)} %broadcast_in_dim.21), calls=%async_computation.4 | async-start | bytes 2097152 | tf_op jit(solution)/shard_map/all_to_all | solution.py:12
  112.0 0.0 copy-done.3
  112.0 0.0 copy-done.4
  112.0 0.0 copy-done.5
  112.0 1.3 convolution_bitcast_fusion
  113.3 9.5 %all-to-all-done.4 = bf16[4,128,1024]{2,1,0:T(8,128)(2,1)S(1)} async-done(((bf16[4,128,1024]{2,1,0:T(8,128)(2,1)}), bf16[4,128,1024]{2,1,0:T(8,128)(2,1)S(1)}, u32[]{:S(2)}, u32[]{:S(2)}) %all-to-all-start.4) | async-done | bytes 1048608 | tf_op jit(solution)/shard_map/all_to_all | solution.py:12
  122.8 0.0 copy-done.1
  122.8 0.5 convolution_bitcast_fusion.1
  123.3 0.0 copy-done
  123.3 0.5 convolution_bitcast_fusion.2
  123.8 0.1 pad_maximum_fusion
  123.9 0.8 constant_dynamic-slice_fusion
  124.8 1.9 collective-permute-start
  126.7 2.2 %collective-permute-done = f32[3,172,256]{2,1,0:T(8,128)} collective-permute-done((f32[3,172,256]{2,1,0:T(8,128)}, f32[3,172,256]{2,1,0:T(8,128)}, u32[]{:S(2)}, u32[]{:S(2)}) %collective-permute-start) | collective-permute-done | bytes 528416 | tf_op jit(solution)/shard_map/ppermute | solution.py:58
  128.9 1.1 add_convert_fusion.1
  130.1 0.1 broadcast_in_dim.42
  130.1 18.9 %all_to_all.48 = bf16[4,3,172,256]{3,2,1,0:T(8,128)(2,1)S(1)} all-to-all(bf16[4,3,172,256]{3,2,1,0:T(8,128)(2,1)S(1)} %broadcast_in_dim.42), channel_id=1, replica_groups=mesh['x'=4,'core'=2,'y'=4,'zh'=8,'zl'=4] {'x'}, dimensions={0} | all-to-all | bytes 2113536 | tf_op jit(solution)/shard_map/all_to_all | solution.py:12
  149.1 0.2 convert_reduce_fusion
  149.2 0.1 multiply_convert_fusion.5
  149.4 2.2 %all_gather.3 = bf16[3,172,512]{2,1,0:T(8,128)(2,1)S(1)} all-gather(bf16[3,172,256]{2,1,0:T(8,128)(2,1)S(1)} %pad_maximum_fusion.1), channel_id=1, replica_groups=mesh['x'=4,'core'=2,'y'=4,'zh'=8,'zl'=4] {'core'}, dimensions={2}, use_global_device_ids=true | all-gather | bytes 792576 | tf_op jit(solution)/shard_map/all_gather | solution.py:61
  151.6 0.5 fusion.1
  152.0 0.5 add_convert_fusion
  152.5 18.1 %all_to_all.49 = bf16[4,128,1024]{2,1,0:T(8,128)(2,1)S(1)} all-to-all(bf16[4,128,1024]{2,1,0:T(8,128)(2,1)S(1)} %bitcast.55), channel_id=1, replica_groups=mesh['x'=4,'core'=2,'y'=4,'zh'=8,'zl'=4] {'y'}, dimensions={0} | all-to-all | bytes 2097152 | tf_op jit(solution)/shard_map/all_to_all | solution.py:12
  170.6 0.2 reduce_sum.56
  170.8 0.2 copy.44
  171.0 0.9 copy.45
  171.8 3.4 %all-to-all-start.7 = ((bf16[4,128,256]{2,1,0:T(8,128)(2,1)}), bf16[4,128,256]{2,1,0:T(8,128)(2,1)S(1)}, u32[]{:S(2)}, u32[]{:S(2)}) async-start(bf16[4,128,256]{2,1,0:T(8,128)(2,1)} %copy.45), calls=%async_computation.7 | async-start | bytes 524288 | tf_op jit(solution)/shard_map/all_to_all | solution.py:12
  175.3 1.1 convolution_convert_fusion.1
  176.4 7.5 %all-to-all-done.7 = bf16[4,128,256]{2,1,0:T(8,128)(2,1)S(1)} async-done(((bf16[4,128,256]{2,1,0:T(8,128)(2,1)}), bf16[4,128,256]{2,1,0:T(8,128)(2,1)S(1)}, u32[]{:S(2)}, u32[]{:S(2)}) %all-to-all-start.7) | async-done | bytes 262176 | tf_op jit(solution)/shard_map/all_to_all | solution.py:12
  183.9 0.6 reshape.60
  184.5 4.2 %all-to-all-start.8 = ((bf16[32,4,256]{2,1,0:T(4,128)(2,1)}), bf16[32,4,256]{2,1,0:T(4,128)(2,1)S(1)}, u32[]{:S(2)}, u32[]{:S(2)}) async-start(bf16[32,4,256]{2,1,0:T(4,128)(2,1)} %reshape.60), calls=%async_computation.8 | async-start | bytes 131072 | tf_op jit(solution)/shard_map/all_to_all | solution.py:12
  188.7 1.1 convolution_convert_fusion.2
  189.8 2.4 %convolution_convert_fusion = bf16[172,1024]{1,0:T(8,128)(2,1)} fusion(bf16[512,1024]{1,0:T(8,128)(2,1)} %param.10, f32[512]{0:T(512)S(1)} %copy-done.5, bf16[3,172,512]{2,1,0:T(8,128)(2,1)S(1)} %all_gather.3), kind=kOutput, calls=%fused_computation.3 | convolution fusion | flops 182104064 | bytes 1583104 | tf_op jit(solution)/shard_map/dot_general | solution.py:83
  192.2 21.1 %all-to-all-done.8 = bf16[32,4,256]{2,1,0:T(4,128)(2,1)S(1)} async-done(((bf16[32,4,256]{2,1,0:T(4,128)(2,1)}), bf16[32,4,256]{2,1,0:T(4,128)(2,1)S(1)}, u32[]{:S(2)}, u32[]{:S(2)}) %all-to-all-start.8) | async-done | bytes 65568 | tf_op jit(solution)/shard_map/all_to_all | solution.py:12
  213.3 1.3 add_convert_fusion.2
  (15 shorter events, 0.3 us)
Async XLA Ops:
  0.6 122.7 %copy-start = (bf16[1024,172]{0,1:T(8,128)(2,1)S(1)}, bf16[1024,172]{0,1:T(8,128)(2,1)}, u32[]{:S(2)}) copy-start(bf16[1024,172]{0,1:T(8,128)(2,1)} %param.11) | copy-start | bytes 1056772
  2.2 17.0 %all-to-all-start = ((bf16[16,16,256]{2,1,0:T(8,128)(2,1)}), bf16[16,16,256]{2,1,0:T(8,128)(2,1)S(1)}, u32[]{:S(2)}, u32[]{:S(2)}) async-start(bf16[16,16,256]{2,1,0:T(8,128)(2,1)} %bitcast.1), calls=%async_computation | async-start | bytes 262144 | tf_op jit(solution)/shard_map/all_to_all | solution.py:12
  107.0 4.9 %copy-start.3 = (bf16[512,1024]{1,0:T(8,128)(2,1)S(1)}, bf16[512,1024]{1,0:T(8,128)(2,1)}, u32[]{:S(2)}) copy-start(bf16[512,1024]{1,0:T(8,128)(2,1)} %param.10) | copy-start | bytes 3145732
  107.0 4.9 %copy-start.4 = (bf16[172,1024]{1,0:T(8,128)(2,1)S(1)}, bf16[172,1024]{1,0:T(8,128)(2,1)}, u32[]{:S(2)}) copy-start(bf16[172,1024]{1,0:T(8,128)(2,1)} %param.13) | copy-start | bytes 1056772
  107.0 4.9 %copy-start.5 = (f32[512]{0:T(512)S(1)}, f32[512]{0:T(512)}, u32[]{:S(2)}) copy-start(f32[512]{0:T(512)} %param.9) | copy-start | bytes 6148
  108.3 14.5 %copy-start.1 = (bf16[1024,172]{0,1:T(8,128)(2,1)S(1)}, bf16[1024,172]{0,1:T(8,128)(2,1)}, u32[]{:S(2)}) copy-start(bf16[1024,172]{0,1:T(8,128)(2,1)} %param.12) | copy-start | bytes 1056772
  108.3 14.5 %all-to-all-start.4 = ((bf16[4,128,1024]{2,1,0:T(8,128)(2,1)}), bf16[4,128,1024]{2,1,0:T(8,128)(2,1)S(1)}, u32[]{:S(2)}, u32[]{:S(2)}) async-start(bf16[4,128,1024]{2,1,0:T(8,128)(2,1)} %broadcast_in_dim.21), calls=%async_computation.4 | async-start | bytes 2097152 | tf_op jit(solution)/shard_map/all_to_all | solution.py:12
  122.8 1.0 copy-start.2
  124.8 4.2 %collective-permute-start = (f32[3,172,256]{2,1,0:T(8,128)}, f32[3,172,256]{2,1,0:T(8,128)}, u32[]{:S(2)}, u32[]{:S(2)}) collective-permute-start(f32[3,172,256]{2,1,0:T(8,128)} %constant_dynamic-slice_fusion), channel_id=1, source_target_pairs={{0,128},{128,0},{1,129},{129,1},{2,130},{130,2},{3,131},{131,3},{4... | collective-permute-start | bytes 1585160 | tf_op jit(solution)/shard_map/ppermute | solution.py:58
  171.8 12.0 %all-to-all-start.7 = ((bf16[4,128,256]{2,1,0:T(8,128)(2,1)}), bf16[4,128,256]{2,1,0:T(8,128)(2,1)S(1)}, u32[]{:S(2)}, u32[]{:S(2)}) async-start(bf16[4,128,256]{2,1,0:T(8,128)(2,1)} %copy.45), calls=%async_computation.7 | async-start | bytes 524288 | tf_op jit(solution)/shard_map/all_to_all | solution.py:12
  184.5 28.7 %all-to-all-start.8 = ((bf16[32,4,256]{2,1,0:T(4,128)(2,1)}), bf16[32,4,256]{2,1,0:T(4,128)(2,1)S(1)}, u32[]{:S(2)}, u32[]{:S(2)}) async-start(bf16[32,4,256]{2,1,0:T(4,128)(2,1)} %reshape.60), calls=%async_computation.8 | async-start | bytes 131072 | tf_op jit(solution)/shard_map/all_to_all | solution.py:12

commit v2 on v1

v2 whole, which is shorter than its diff:
```python
import jax
import jax.numpy as jnp
from jax import lax
from jax.sharding import Mesh
from jax.sharding import PartitionSpec as P

BF = jnp.bfloat16
F32 = jnp.float32


def dot(a, b, i, j):
    return lax.dot_general(a, b, (((i,), (j,)), ((), ())), preferred_element_type=F32)


def exchange(x, axis):
    return lax.all_to_all(x, axis, 0, 0, tiled=True)


def to_all(x, axis, count):
    return exchange(jnp.broadcast_to(x[None], (count,) + x.shape), axis)


def cut_lanes(x, count):
    width = x.shape[1] // count
    return jnp.stack([x[:, i * width : (i + 1) * width] for i in range(count)])


def join_lanes(x):
    return jnp.concatenate([x[i] for i in range(x.shape[0])], axis=1)


def add_up(x):
    total = x[0].astype(F32)
    for i in range(1, x.shape[0]):
        total = total + x[i].astype(F32)
    return total


def all_tokens_of_y(tokens):
    nh, nl = lax.axis_size("zh"), lax.axis_size("zl")
    here, width = tokens.shape
    cut = cut_lanes(tokens, nl)
    cut = jnp.broadcast_to(cut[None], (nh,) + cut.shape).reshape(nh * nl, here, width // nl)
    return exchange(cut, ("zh", "zl")).reshape(nh * nl * here, width // nl)


def gather_routed(held, route_index):
    ny, nl = lax.axis_size("y"), lax.axis_size("zl")
    count, quarter = held.shape
    rows = route_index.shape[0]
    place = route_index - lax.axis_index("y") * count
    pick = (place[:, None] == lax.broadcasted_iota(jnp.int32, (rows, count), 1)).astype(BF)
    filled = jnp.dot(pick, held, preferred_element_type=F32).astype(BF)
    got = add_up(exchange(filled.reshape(ny, rows // ny, quarter), "y")).astype(BF)
    got = join_lanes(to_all(got, "zl", nl))
    return to_all(got, "y", ny).reshape(rows, nl * quarter)


def activate(gate, up, back):
    sig = jax.nn.sigmoid(gate)
    silu = gate * sig
    hidden = (silu * up).astype(BF)
    grad_up = (back * silu).astype(BF)
    grad_gate = (back * up * sig * (1.0 + gate * (1.0 - sig))).astype(BF)
    return (hidden, grad_gate, grad_up)


def chip_sum(part):
    half = part.shape[1] // lax.axis_size("core")
    core = lax.axis_index("core")
    keep = lax.dynamic_slice_in_dim(part, core * half, half, 1)
    give = lax.dynamic_slice_in_dim(part, (1 - core) * half, half, 1)
    return keep + lax.ppermute(give, "core", [(0, 1), (1, 0)])


def sum_by_pairs(part):
    part = part + lax.ppermute(part, "x", [(0, 1), (1, 0), (2, 3), (3, 2)])
    return part + lax.ppermute(part, "x", [(0, 3), (3, 0), (1, 2), (2, 1)])


def scatter_rows(total, out_grad):
    rows, width = total.shape
    ny, nh, nl = lax.axis_size("y"), lax.axis_size("zh"), lax.axis_size("zl")
    slots, quarter = rows // ny, width // nl
    each = slots // (nh * nl)
    part = add_up(exchange(total.reshape(ny, slots, width), "y")).astype(BF)
    part = add_up(exchange(cut_lanes(part, nl), "zl")).astype(BF)
    part = exchange(part.reshape(nh * nl, each, quarter), ("zh", "zl"))
    part = join_lanes(add_up(part.reshape(nh, nl, each, quarter)))
    first = lax.axis_index(("y", "zh", "zl")) * each
    mine = lax.dynamic_slice_in_dim(out_grad, first, each, 0)
    return (mine.astype(F32) + part).astype(BF)


def body(tokens, route_index, router_score, out_grad, gate_weight, up_weight, down_weight):
    units = down_weight.shape[0]
    padded = (units + 15) // 16 * 16
    more = ((0, padded - units), (0, 0))
    both = jnp.concatenate([jnp.pad(gate_weight.T, more), jnp.pad(up_weight.T, more)])
    held = all_tokens_of_y(tokens)
    scaled = (router_score[:, None] * out_grad.astype(F32)).astype(BF)
    back = sum_by_pairs(chip_sum(dot(jnp.pad(down_weight, more), scaled, 1, 1)))
    held, back, both = lax.optimization_barrier((held, back, both))
    routed = gather_routed(held, route_index)
    sums = add_up(to_all(chip_sum(dot(both, routed, 1, 1)).astype(BF), "x", lax.axis_size("x")))
    grads = jnp.stack(activate(sums[:padded], sums[padded:], back))
    grads = lax.all_gather(grads, "core", axis=2, tiled=True)
    total = dot(grads[1:].reshape(2 * padded, -1), both, 0, 0)
    d_rows = scatter_rows(total.astype(BF), out_grad)
    d_down = dot(grads[0, :units], scaled, 1, 0).astype(BF)
    d_gate = dot(routed, grads[1, :units], 0, 1).astype(BF)
    d_up = dot(routed, grads[2, :units], 0, 1).astype(BF)
    return (d_rows, d_gate, d_up, d_down)


def solution(mesh):
    rows, cols = mesh.devices.shape
    fine = Mesh(mesh.devices.reshape(rows // 2, 2, 4, cols // 16, 4), ("x", "core", "y", "zh", "zl"))
    row, col = ("x", "core"), ("y", "zh", "zl")
    placed = (
        P(col, row),
        P(),
        P(),
        P(None, row),
        P(row, col),
        P(row, col),
        P(col, row),
    )
    return jax.shard_map(
        body,
        mesh=fine,
        in_specs=placed,
        out_specs=(P(col, row), P(row, col), P(row, col), P(col, row)),
        check_vma=False,
    )
```

time: 215 us -> 193 us (0.90)
  blocking collectives: 127 us -> 69.1 us
  starting transfers between devices: 21.8 us -> 47 us
  waiting for transfers between devices: 47.9 us -> 63.9 us
  local copies, waits for them, and re-layouts: 5.57 us -> 2.46 us
    all_to_all x5, blocking collectives: 124 us -> 66.9 us  [exchange(): return lax.all_to_all(x, axis, 0, 0, tiled=True)]
    all_to_all x4 -> x3, starting transfers between devices: 19.8 us -> 37.3 us  [exchange(): return lax.all_to_all(x, axis, 0, 0, tiled=True)]
    ppermute x1 -> x4, waiting for transfers between devices: 2.24 us -> 13.2 us  [the longest x1 5.96 us: sum_by_pairs(): part = part + lax.ppermute(part, 'x', [(0, 1), (1, 0), (2, 3), (3, 2)])]
    ppermute x1 -> x4, starting transfers between devices: 1.91 us -> 9.68 us  [the longest x2 3.84 us: chip_sum(): return keep + lax.ppermute(give, 'core', [(0, 1), (1, 0)])]
    all_to_all x4 -> x3, waiting for transfers between devices: 45.7 us -> 50.7 us  [exchange(): return lax.all_to_all(x, axis, 0, 0, tiled=True)]
    dot_general x8 -> x6, matrix products: 7.84 us -> 6.61 us  [dot(): lax.dot_general(a, b, (((i,), (j,)), ((), ())), preferred_element_type=F32)]
  transfers between devices with their start and end apart: 5 -> 7, of which waited for: 5 -> 7; matrix products, arithmetic and copies ran while one was open for 3% -> 3% of each run, Pallas kernels for 0% -> 0%
where the time goes in v2:
time: 193 us; the launch traced here: 192 us
  blocking collectives  69.1 us (36%)
  waiting for transfers between devices  63.9 us (33%)
  starting transfers between devices  47 us (24%)
  matrix products  6.97 us (4%)
  local copies, waits for them, and re-layouts  2.46 us (1%)
  other arithmetic  2.08 us (1%)
    all_to_all x5, blocking collectives, exchange(): return lax.all_to_all(x, axis, 0, 0, tiled=True)  66.9 us
    all_to_all x3, waiting for transfers between devices, exchange(): return lax.all_to_all(x, axis, 0, 0, tiled=True)  50.7 us
    all_to_all x3, starting transfers between devices, exchange(): return lax.all_to_all(x, axis, 0, 0, tiled=True)  37.3 us
    dot_general x6, matrix products, dot(): lax.dot_general(a, b, (((i,), (j,)), ((), ())), preferred_element_type=F32)  6.61 us
    ppermute x1, waiting for transfers between devices, sum_by_pairs(): part = part + lax.ppermute(part, 'x', [(0, 1), (1, 0), (2, 3), (3, 2)])  5.96 us
    ppermute x1, waiting for transfers between devices, sum_by_pairs(): return part + lax.ppermute(part, 'x', [(0, 3), (3, 0), (1, 2), (2, 1)])  4.23 us
  transfers between devices with their start and end apart: 7, of which 7 were waited for; matrix products, arithmetic and copies ran while one was open for 3% of the time, Pallas kernels for 0%

profile of v2, /device:TPU:2, one launch (start us, length us, event | category | flops | bytes accessed | tf_op | source)
XLA Modules:
  0.0 192.5 jit_solution(484701953348227780)
XLA Ops:
  0.6 0.8 slice_bitcast_fusion.19
  1.4 0.7 broadcast_in_dim.10
  2.1 28.7 %all-to-all-start = ((bf16[32,16,256]{2,1,0:T(8,128)(2,1)}), bf16[32,16,256]{2,1,0:T(8,128)(2,1)S(1)}, u32[]{:S(2)}, u32[]{:S(2)}) async-start(bf16[32,16,256]{2,1,0:T(8,128)(2,1)} %bitcast.4), calls=%async_computation | async-start | bytes 524288 | tf_op jit(solution)/shard_map/all_to_all | solution.py:16
  30.9 0.0 copy-start
  30.9 0.0 copy-start.1
  30.9 1.9 %fusion.4 = f32[176,512]{1,0:T(8,128)S(1)} fusion(bf16[512,1024]{1,0:T(8,128)(2,1)} %param.10, f32[512]{0:T(512)} %param.9, bf16[172,1024]{1,0:T(8,128)(2,1)} %param.13), kind=kOutput, calls=%fused_computation.14 | convolution fusion | flops 186122240 | bytes 1763328 | tf_op jit(solution)/shard_map/dot_general | solution.py:12
  32.8 1.9 collective-permute-start
  34.8 1.4 collective-permute-done
  36.2 0.0 copy-start.2
  36.2 2.4 %collective-permute-start.1 = (f32[176,256]{1,0:T(8,128)S(1)}, f32[176,256]{1,0:T(8,128)S(1)}, u32[]{:S(2)}, u32[]{:S(2)}) collective-permute-start(f32[176,256]{1,0:T(8,128)S(1)} %dynamic-slice_add_fusion), channel_id=1, source_target_pairs={{0,256},{256,0},{512,768},{768,512},{1,257},{257,1},{513,769},{769... | collective-permute-start | bytes 540680 | tf_op jit(solution)/shard_map/ppermute | solution.py:77
  38.7 0.0 copy-done
  38.7 0.0 copy-done.1
  38.7 0.1 fusion.2
  38.7 6.0 %collective-permute-done.1 = f32[176,256]{1,0:T(8,128)S(1)} collective-permute-done((f32[176,256]{1,0:T(8,128)S(1)}, f32[176,256]{1,0:T(8,128)S(1)}, u32[]{:S(2)}, u32[]{:S(2)}) %collective-permute-start.1) | collective-permute-done | bytes 180256 | tf_op jit(solution)/shard_map/ppermute | solution.py:77
  44.7 3.4 %collective-permute-start.2 = (f32[176,256]{1,0:T(8,128)S(1)}, f32[176,256]{1,0:T(8,128)S(1)}, u32[]{:S(2)}, u32[]{:S(2)}) collective-permute-start(f32[176,256]{1,0:T(8,128)S(1)} %add.126), channel_id=1, source_target_pairs={{0,768},{768,0},{256,512},{512,256},{1,769},{769,1},{257,513},{513... | collective-permute-start | bytes 540680 | tf_op jit(solution)/shard_map/ppermute | solution.py:78
  48.1 0.0 copy-done.2
  48.2 4.2 %collective-permute-done.2 = f32[176,256]{1,0:T(8,128)S(1)} collective-permute-done((f32[176,256]{1,0:T(8,128)S(1)}, f32[176,256]{1,0:T(8,128)S(1)}, u32[]{:S(2)}, u32[]{:S(2)}) %collective-permute-start.2) | collective-permute-done | bytes 180256 | tf_op jit(solution)/shard_map/ppermute | solution.py:78
  52.4 21.0 %all-to-all-done = bf16[32,16,256]{2,1,0:T(8,128)(2,1)S(1)} async-done(((bf16[32,16,256]{2,1,0:T(8,128)(2,1)}), bf16[32,16,256]{2,1,0:T(8,128)(2,1)S(1)}, u32[]{:S(2)}, u32[]{:S(2)}) %all-to-all-start) | async-done | bytes 262176 | tf_op jit(solution)/shard_map/all_to_all | solution.py:16
  73.4 0.4 convolution_convert_fusion.4
  73.8 10.9 %all_to_all.40 = bf16[4,128,256]{2,1,0:T(8,128)(2,1)S(1)} all-to-all(bf16[4,128,256]{2,1,0:T(8,128)(2,1)S(1)} %bitcast.96), channel_id=1, replica_groups=mesh['x'=4,'core'=2,'y'=4,'zh'=8,'zl'=4] {'y'}, dimensions={0} | all-to-all | bytes 524288 | tf_op jit(solution)/shard_map/all_to_all | solution.py:16
  84.8 9.5 %all_to_all.41 = bf16[4,128,256]{2,1,0:T(8,128)(2,1)S(1)} all-to-all(bf16[4,128,256]{2,1,0:T(8,128)(2,1)S(1)} %broadcast_in_dim.12), channel_id=1, replica_groups=mesh['x'=4,'core'=2,'y'=4,'zh'=8,'zl'=4] {'zl'}, dimensions={0} | all-to-all | bytes 524288 | tf_op jit(solution)/shard_map/all_to_all | solution.py:16
  94.3 0.1 broadcast_in_dim.13
  94.5 13.3 %all_to_all.42 = bf16[4,128,1024]{2,1,0:T(8,128)(2,1)S(1)} all-to-all(bf16[4,128,1024]{2,1,0:T(8,128)(2,1)S(1)} %broadcast_in_dim.13), channel_id=1, replica_groups=mesh['x'=4,'core'=2,'y'=4,'zh'=8,'zl'=4] {'y'}, dimensions={0} | all-to-all | bytes 2097152 | tf_op jit(solution)/shard_map/all_to_all | solution.py:16
  107.8 0.6 fusion.14
  108.4 1.9 collective-permute-start.3
  110.3 1.6 collective-permute-done.3
  112.0 0.1 add_convert_fusion.1
  112.1 15.1 %all_to_all.43 = bf16[4,352,256]{2,1,0:T(8,128)(2,1)S(1)} all-to-all(bf16[4,352,256]{2,1,0:T(8,128)(2,1)S(1)} %broadcast_in_dim.14), channel_id=1, replica_groups=mesh['x'=4,'core'=2,'y'=4,'zh'=8,'zl'=4] {'x'}, dimensions={0} | all-to-all | bytes 1441792 | tf_op jit(solution)/shard_map/all_to_all | solution.py:16
  127.2 0.1 convert_add_fusion
  127.2 0.1 fusion.10
  127.4 2.2 %all_gather.3 = bf16[3,176,512]{2,1,0:T(8,128)(2,1)S(1)} all-gather(bf16[3,176,256]{2,1,0:T(8,128)(2,1)S(1)} %pad_maximum_fusion), channel_id=1, replica_groups=mesh['x'=4,'core'=2,'y'=4,'zh'=8,'zl'=4] {'core'}, dimensions={2}, use_global_device_ids=true | all-gather | bytes 811008 | tf_op jit(solution)/shard_map/all_gather | solution.py:107
  129.6 0.7 convolution_convert_fusion
  130.4 18.1 %all_to_all.44 = bf16[4,128,1024]{2,1,0:T(8,128)(2,1)S(1)} all-to-all(bf16[4,128,1024]{2,1,0:T(8,128)(2,1)S(1)} %bitcast.91), channel_id=1, replica_groups=mesh['x'=4,'core'=2,'y'=4,'zh'=8,'zl'=4] {'y'}, dimensions={0} | all-to-all | bytes 2097152 | tf_op jit(solution)/shard_map/all_to_all | solution.py:16
  148.5 0.2 fusion.6
  148.7 0.7 pad_maximum_fusion.2
  149.4 3.4 %all-to-all-start.6 = ((bf16[4,128,256]{2,1,0:T(8,128)(2,1)}), bf16[4,128,256]{2,1,0:T(8,128)(2,1)S(1)}, u32[]{:S(2)}, u32[]{:S(2)}) async-start(bf16[4,128,256]{2,1,0:T(8,128)(2,1)} %pad_maximum_fusion.2), calls=%async_computation.6 | async-start | bytes 524288 | tf_op jit(solution)/shard_map/all_to_all | solution.py:16
  152.8 1.1 convolution_convert_fusion.2
  153.9 0.0 copy-start.3
  153.9 0.0 copy-start.4
  153.9 7.5 %all-to-all-done.6 = bf16[4,128,256]{2,1,0:T(8,128)(2,1)S(1)} async-done(((bf16[4,128,256]{2,1,0:T(8,128)(2,1)}), bf16[4,128,256]{2,1,0:T(8,128)(2,1)S(1)}, u32[]{:S(2)}, u32[]{:S(2)}) %all-to-all-start.6) | async-done | bytes 262176 | tf_op jit(solution)/shard_map/all_to_all | solution.py:16
  161.5 0.6 add.144
  162.1 5.2 %all-to-all-start.7 = ((bf16[32,4,256]{2,1,0:T(4,128)(2,1)}), bf16[32,4,256]{2,1,0:T(4,128)(2,1)S(1)}, u32[]{:S(2)}, u32[]{:S(2)}) async-start(bf16[32,4,256]{2,1,0:T(4,128)(2,1)} %add.144), calls=%async_computation.7 | async-start | bytes 131072 | tf_op jit(solution)/shard_map/all_to_all | solution.py:16
  167.3 1.1 convolution_convert_fusion.3
  168.4 0.0 copy-done.3
  168.4 0.0 copy-done.4
  168.4 1.2 convolution_convert_fusion.1
  169.6 22.2 %all-to-all-done.7 = bf16[32,4,256]{2,1,0:T(4,128)(2,1)S(1)} async-done(((bf16[32,4,256]{2,1,0:T(4,128)(2,1)}), bf16[32,4,256]{2,1,0:T(4,128)(2,1)S(1)}, u32[]{:S(2)}, u32[]{:S(2)}) %all-to-all-start.7) | async-done | bytes 65568 | tf_op jit(solution)/shard_map/all_to_all | solution.py:16
  191.8 0.6 fusion.12
  (18 shorter events, 0.4 us)
Async XLA Ops:
  2.1 71.3 %all-to-all-start = ((bf16[32,16,256]{2,1,0:T(8,128)(2,1)}), bf16[32,16,256]{2,1,0:T(8,128)(2,1)S(1)}, u32[]{:S(2)}, u32[]{:S(2)}) async-start(bf16[32,16,256]{2,1,0:T(8,128)(2,1)} %bitcast.4), calls=%async_computation | async-start | bytes 524288 | tf_op jit(solution)/shard_map/all_to_all | solution.py:16
  30.9 7.8 %copy-start = (bf16[1024,172]{0,1:T(8,128)(2,1)S(1)}, bf16[1024,172]{0,1:T(8,128)(2,1)}, u32[]{:S(2)}) copy-start(bf16[1024,172]{0,1:T(8,128)(2,1)} %param.12) | copy-start | bytes 1056772
  30.9 7.8 %copy-start.1 = (bf16[1024,172]{0,1:T(8,128)(2,1)S(1)}, bf16[1024,172]{0,1:T(8,128)(2,1)}, u32[]{:S(2)}) copy-start(bf16[1024,172]{0,1:T(8,128)(2,1)} %param.11) | copy-start | bytes 1056772
  32.8 3.3 %collective-permute-start = (f32[176,256]{1,0:T(8,128)S(1)}, f32[176,256]{1,0:T(8,128)S(1)}, u32[]{:S(2)}, u32[]{:S(2)}) collective-permute-start(f32[176,256]{1,0:T(8,128)S(1)} %constant_dynamic-slice_fusion.1), channel_id=1, source_target_pairs={{0,128},{128,0},{1,129},{129,1},{2,130},{130,2},{3,131},{131,3},{4... | collective-permute-start | bytes 540680 | tf_op jit(solution)/shard_map/ppermute | solution.py:73
  36.2 11.9 %copy-start.2 = (s32[512]{0:T(512)S(1)}, s32[512]{0:T(512)}, u32[]{:S(2)}) copy-start(s32[512]{0:T(512)} %param.8) | copy-start | bytes 6148
  36.2 8.5 %collective-permute-start.1 = (f32[176,256]{1,0:T(8,128)S(1)}, f32[176,256]{1,0:T(8,128)S(1)}, u32[]{:S(2)}, u32[]{:S(2)}) collective-permute-start(f32[176,256]{1,0:T(8,128)S(1)} %dynamic-slice_add_fusion), channel_id=1, source_target_pairs={{0,256},{256,0},{512,768},{768,512},{1,257},{257,1},{513,769},{769... | collective-permute-start | bytes 540680 | tf_op jit(solution)/shard_map/ppermute | solution.py:77
  44.7 7.7 %collective-permute-start.2 = (f32[176,256]{1,0:T(8,128)S(1)}, f32[176,256]{1,0:T(8,128)S(1)}, u32[]{:S(2)}, u32[]{:S(2)}) collective-permute-start(f32[176,256]{1,0:T(8,128)S(1)} %add.126), channel_id=1, source_target_pairs={{0,768},{768,0},{256,512},{512,256},{1,769},{769,1},{257,513},{513... | collective-permute-start | bytes 540680 | tf_op jit(solution)/shard_map/ppermute | solution.py:78
  108.4 3.6 %collective-permute-start.3 = (f32[352,256]{1,0:T(8,128)S(1)}, f32[352,256]{1,0:T(8,128)S(1)}, u32[]{:S(2)}, u32[]{:S(2)}) collective-permute-start(f32[352,256]{1,0:T(8,128)S(1)} %constant_dynamic-slice_fusion), channel_id=1, source_target_pairs={{0,128},{128,0},{1,129},{129,1},{2,130},{130,2},{3,131},{131,3},{4... | collective-permute-start | bytes 1081352 | tf_op jit(solution)/shard_map/ppermute | solution.py:73
  149.4 12.0 %all-to-all-start.6 = ((bf16[4,128,256]{2,1,0:T(8,128)(2,1)}), bf16[4,128,256]{2,1,0:T(8,128)(2,1)S(1)}, u32[]{:S(2)}, u32[]{:S(2)}) async-start(bf16[4,128,256]{2,1,0:T(8,128)(2,1)} %pad_maximum_fusion.2), calls=%async_computation.6 | async-start | bytes 524288 | tf_op jit(solution)/shard_map/all_to_all | solution.py:16
  153.9 14.5 %copy-start.3 = (bf16[512,1024]{1,0:T(8,128)(2,1)S(1)}, bf16[512,1024]{1,0:T(8,128)(2,1)}, u32[]{:S(2)}) copy-start(bf16[512,1024]{1,0:T(8,128)(2,1)} %param.10) | copy-start | bytes 3145732
  153.9 14.5 %copy-start.4 = (f32[512]{0:T(512)S(1)}, f32[512]{0:T(512)}, u32[]{:S(2)}) copy-start(f32[512]{0:T(512)} %param.9) | copy-start | bytes 6148
  162.1 29.7 %all-to-all-start.7 = ((bf16[32,4,256]{2,1,0:T(4,128)(2,1)}), bf16[32,4,256]{2,1,0:T(4,128)(2,1)S(1)}, u32[]{:S(2)}, u32[]{:S(2)}) async-start(bf16[32,4,256]{2,1,0:T(4,128)(2,1)} %add.144), calls=%async_computation.7 | async-start | bytes 131072 | tf_op jit(solution)/shard_map/all_to_all | solution.py:16

commit v3 on v2

--- a/solution.py
+++ b/solution.py
@@ -6,6 +6,7 @@
 
 BF = jnp.bfloat16
 F32 = jnp.float32
+Z = ("za", "zb", "zc")
 
 
 def dot(a, b, i, j):
@@ -21,12 +22,14 @@
 
 
 def cut_lanes(x, count):
-    width = x.shape[1] // count
-    return jnp.stack([x[:, i * width : (i + 1) * width] for i in range(count)])
+    rows, width = x.shape
+    part = width // count
+    return x.reshape(rows // 8, 8, count, part).transpose(2, 0, 1, 3).reshape(count, rows, part)
 
 
 def join_lanes(x):
-    return jnp.concatenate([x[i] for i in range(x.shape[0])], axis=1)
+    count, rows, part = x.shape
+    return x.reshape(count, rows // 8, 8, part).transpose(1, 2, 0, 3).reshape(rows, count * part)
 
 
 def add_up(x):
@@ -37,23 +40,23 @@
 
 
 def all_tokens_of_y(tokens):
-    nh, nl = lax.axis_size("zh"), lax.axis_size("zl")
+    nh, nl = lax.axis_size("za"), lax.axis_size("zb") * lax.axis_size("zc")
     here, width = tokens.shape
     cut = cut_lanes(tokens, nl)
     cut = jnp.broadcast_to(cut[None], (nh,) + cut.shape).reshape(nh * nl, here, width // nl)
-    return exchange(cut, ("zh", "zl")).reshape(nh * nl * here, width // nl)
+    return exchange(cut, Z).reshape(nh * nl * here, width // nl)
 
 
 def gather_routed(held, route_index):
-    ny, nl = lax.axis_size("y"), lax.axis_size("zl")
-    count, quarter = held.shape
+    ny, nl = lax.axis_size("y"), lax.axis_size("zb") * lax.axis_size("zc")
+    count, share = held.shape
     rows = route_index.shape[0]
     place = route_index - lax.axis_index("y") * count
     pick = (place[:, None] == lax.broadcasted_iota(jnp.int32, (rows, count), 1)).astype(BF)
     filled = jnp.dot(pick, held, preferred_element_type=F32).astype(BF)
-    got = add_up(exchange(filled.reshape(ny, rows // ny, quarter), "y")).astype(BF)
-    got = join_lanes(to_all(got, "zl", nl))
-    return to_all(got, "y", ny).reshape(rows, nl * quarter)
+    got = add_up(exchange(filled.reshape(ny, rows // ny, share), "y")).astype(BF)
+    got = join_lanes(to_all(got, ("zb", "zc"), nl))
+    return to_all(got, "y", ny).reshape(rows, nl * share)
 
 
 def activate(gate, up, back):
@@ -80,14 +83,15 @@
 
 def scatter_rows(total, out_grad):
     rows, width = total.shape
-    ny, nh, nl = lax.axis_size("y"), lax.axis_size("zh"), lax.axis_size("zl")
+    ny, nh, nl = lax.axis_size("y"), lax.axis_size("za") * lax.axis_size("zb"), lax.axis_size("zc")
     slots, quarter = rows // ny, width // nl
     each = slots // (nh * nl)
     part = add_up(exchange(total.reshape(ny, slots, width), "y")).astype(BF)
-    part = add_up(exchange(cut_lanes(part, nl), "zl")).astype(BF)
-    part = exchange(part.reshape(nh * nl, each, quarter), ("zh", "zl"))
-    part = join_lanes(add_up(part.reshape(nh, nl, each, quarter)))
-    first = lax.axis_index(("y", "zh", "zl")) * each
+    part = jnp.stack([part[:, i * quarter : (i + 1) * quarter] for i in range(nl)])
+    part = add_up(exchange(part, "zc")).astype(BF)
+    part = exchange(part.reshape(nh * nl, each, quarter), Z)
+    part = add_up(part.reshape(nh, nl, each, quarter)).transpose(1, 0, 2).reshape(each, width)
+    first = lax.axis_index(("y",) + Z) * each
     mine = lax.dynamic_slice_in_dim(out_grad, first, each, 0)
     return (mine.astype(F32) + part).astype(BF)
 
@@ -115,8 +119,8 @@
 
 def solution(mesh):
     rows, cols = mesh.devices.shape
-    fine = Mesh(mesh.devices.reshape(rows // 2, 2, 4, cols // 16, 4), ("x", "core", "y", "zh", "zl"))
-    row, col = ("x", "core"), ("y", "zh", "zl")
+    fine = Mesh(mesh.devices.reshape(rows // 2, 2, 4, cols // 32, 2, 4), ("x", "core", "y") + Z)
+    row, col = ("x", "core"), ("y",) + Z
     placed = (
         P(col, row),
         P(),

time: 193 us -> 199 us (1.031)
  waiting for transfers between devices: 63.9 us -> 53.4 us
  starting transfers between devices: 47 us -> 56.4 us
  blocking collectives: 69.1 us -> 76.1 us
    all_to_all x3, waiting for transfers between devices: 50.7 us -> 40.1 us  [exchange(): return lax.all_to_all(x, axis, 0, 0, tiled=True)]
    all_to_all x3, starting transfers between devices: 37.3 us -> 46.8 us  [exchange(): return lax.all_to_all(x, axis, 0, 0, tiled=True)]
    all_to_all x5, blocking collectives: 66.9 us -> 74 us  [exchange(): return lax.all_to_all(x, axis, 0, 0, tiled=True)]
where the time goes in v3:
time: 199 us; the launch traced here: 198 us
  blocking collectives  76.1 us (38%)
  starting transfers between devices  56.4 us (28%)
  waiting for transfers between devices  53.4 us (27%)
  matrix products  6.96 us (3%)
  local copies, waits for them, and re-layouts  2.64 us (1%)
  other arithmetic  2.04 us (1%)
    all_to_all x5, blocking collectives, exchange(): return lax.all_to_all(x, axis, 0, 0, tiled=True)  74 us
    all_to_all x3, starting transfers between devices, exchange(): return lax.all_to_all(x, axis, 0, 0, tiled=True)  46.8 us
    all_to_all x3, waiting for transfers between devices, exchange(): return lax.all_to_all(x, axis, 0, 0, tiled=True)  40.1 us
    dot_general x6, matrix products, dot(): lax.dot_general(a, b, (((i,), (j,)), ((), ())), preferred_element_type=F32)  6.61 us
    ppermute x1, waiting for transfers between devices, sum_by_pairs(): part = part + lax.ppermute(part, 'x', [(0, 1), (1, 0), (2, 3), (3, 2)])  5.96 us
    ppermute x1, waiting for transfers between devices, sum_by_pairs(): return part + lax.ppermute(part, 'x', [(0, 3), (3, 0), (1, 2), (2, 1)])  4.23 us
  transfers between devices with their start and end apart: 7, of which 7 were waited for; matrix products, arithmetic and copies ran while one was open for 3% of the time, Pallas kernels for 0%

profile of v3, /device:TPU:2, one launch (start us, length us, event | category | flops | bytes accessed | tf_op | source)
XLA Modules:
  0.0 198.5 jit_solution(9992169958982214450)
XLA Ops:
  0.6 0.8 copy.25
  1.4 0.7 broadcast_in_dim.15
  2.1 28.7 %all-to-all-start = ((bf16[32,16,128]{2,1,0:T(8,128)(2,1)}), bf16[32,16,128]{2,1,0:T(8,128)(2,1)S(1)}, u32[]{:S(2)}, u32[]{:S(2)}) async-start(bf16[32,16,128]{2,1,0:T(8,128)(2,1)} %bitcast.2), calls=%async_computation | async-start | bytes 262144 | tf_op jit(solution)/shard_map/all_to_all | solution.py:17
  30.8 0.0 copy-start
  30.8 0.0 copy-start.1
  30.8 1.9 fusion.4
  32.8 1.9 collective-permute-start
  34.7 1.4 collective-permute-done
  36.1 0.0 copy-start.2
  36.2 2.4 %collective-permute-start.1 = (f32[176,256]{1,0:T(8,128)S(1)}, f32[176,256]{1,0:T(8,128)S(1)}, u32[]{:S(2)}, u32[]{:S(2)}) collective-permute-start(f32[176,256]{1,0:T(8,128)S(1)} %dynamic-slice_add_fusion), channel_id=1, source_target_pairs={{0,256},{256,0},{512,768},{768,512},{1,257},{257,1},{513,769},{769... | collective-permute-start | bytes 540680 | tf_op jit(solution)/shard_map/ppermute | solution.py:80
  38.6 0.0 copy-done
  38.6 0.0 copy-done.1
  38.6 0.1 fusion.2
  38.7 6.0 %collective-permute-done.1 = f32[176,256]{1,0:T(8,128)S(1)} collective-permute-done((f32[176,256]{1,0:T(8,128)S(1)}, f32[176,256]{1,0:T(8,128)S(1)}, u32[]{:S(2)}, u32[]{:S(2)}) %collective-permute-start.1) | collective-permute-done | bytes 180256 | tf_op jit(solution)/shard_map/ppermute | solution.py:80
  44.7 3.4 %collective-permute-start.2 = (f32[176,256]{1,0:T(8,128)S(1)}, f32[176,256]{1,0:T(8,128)S(1)}, u32[]{:S(2)}, u32[]{:S(2)}) collective-permute-start(f32[176,256]{1,0:T(8,128)S(1)} %add.130), channel_id=1, source_target_pairs={{0,768},{768,0},{256,512},{512,256},{1,769},{769,1},{257,513},{513... | collective-permute-start | bytes 540680 | tf_op jit(solution)/shard_map/ppermute | solution.py:81
  48.1 0.0 copy-done.2
  48.1 4.2 %collective-permute-done.2 = f32[176,256]{1,0:T(8,128)S(1)} collective-permute-done((f32[176,256]{1,0:T(8,128)S(1)}, f32[176,256]{1,0:T(8,128)S(1)}, u32[]{:S(2)}, u32[]{:S(2)}) %collective-permute-start.2) | collective-permute-done | bytes 180256 | tf_op jit(solution)/shard_map/ppermute | solution.py:81
  52.4 9.9 %all-to-all-done = bf16[32,16,128]{2,1,0:T(8,128)(2,1)S(1)} async-done(((bf16[32,16,128]{2,1,0:T(8,128)(2,1)}), bf16[32,16,128]{2,1,0:T(8,128)(2,1)S(1)}, u32[]{:S(2)}, u32[]{:S(2)}) %all-to-all-start) | async-done | bytes 131104 | tf_op jit(solution)/shard_map/all_to_all | solution.py:17
  62.3 0.4 convolution_convert_fusion.4
  62.6 10.2 %all_to_all.40 = bf16[4,128,128]{2,1,0:T(8,128)(2,1)S(1)} all-to-all(bf16[4,128,128]{2,1,0:T(8,128)(2,1)S(1)} %bitcast.99), channel_id=1, replica_groups=mesh['x'=4,'core'=2,'y'=4,'za'=4,'zb'=2,'zc'=4] {'y'}, dimensions={0} | all-to-all | bytes 262144 | tf_op jit(solution)/shard_map/all_to_all | solution.py:17
  72.9 17.2 %all_to_all.41 = bf16[8,128,128]{2,1,0:T(8,128)(2,1)S(1)} all-to-all(bf16[8,128,128]{2,1,0:T(8,128)(2,1)S(1)} %broadcast_in_dim.33), channel_id=1, replica_groups=mesh['x'=4,'core'=2,'y'=4,'za'=4,'zb'=2,'zc'=4] {'zb','zc'}, dimensions={0} | all-to-all | bytes 524288 | tf_op jit(solution)/shard_map/all_to_all | solution.py:17
  90.2 0.2 copy.24
  90.4 0.1 broadcast_in_dim.35
  90.5 13.3 %all_to_all.42 = bf16[4,128,1024]{2,1,0:T(8,128)(2,1)S(1)} all-to-all(bf16[4,128,1024]{2,1,0:T(8,128)(2,1)S(1)} %broadcast_in_dim.35), channel_id=1, replica_groups=mesh['x'=4,'core'=2,'y'=4,'za'=4,'zb'=2,'zc'=4] {'y'}, dimensions={0} | all-to-all | bytes 2097152 | tf_op jit(solution)/shard_map/all_to_all | solution.py:17
  103.8 0.6 fusion.13
  104.5 1.9 collective-permute-start.3
  106.4 1.6 collective-permute-done.3
  108.0 0.1 add_convert_fusion.1
  108.1 15.1 %all_to_all.43 = bf16[4,352,256]{2,1,0:T(8,128)(2,1)S(1)} all-to-all(bf16[4,352,256]{2,1,0:T(8,128)(2,1)S(1)} %broadcast_in_dim.36), channel_id=1, replica_groups=mesh['x'=4,'core'=2,'y'=4,'za'=4,'zb'=2,'zc'=4] {'x'}, dimensions={0} | all-to-all | bytes 1441792 | tf_op jit(solution)/shard_map/all_to_all | solution.py:17
  123.2 0.1 convert_add_fusion
  123.3 0.1 fusion.10
  123.5 2.2 %all_gather.3 = bf16[3,176,512]{2,1,0:T(8,128)(2,1)S(1)} all-gather(bf16[3,176,256]{2,1,0:T(8,128)(2,1)S(1)} %pad_maximum_fusion), channel_id=1, replica_groups=mesh['x'=4,'core'=2,'y'=4,'za'=4,'zb'=2,'zc'=4] {'core'}, dimensions={2}, use_global_device_ids=true | all-gather | bytes 811008 | tf_op jit(solution)/shard_map/all_gather | solution.py:111
  125.7 0.7 convolution_convert_fusion
  126.4 18.1 %all_to_all.44 = bf16[4,128,1024]{2,1,0:T(8,128)(2,1)S(1)} all-to-all(bf16[4,128,1024]{2,1,0:T(8,128)(2,1)S(1)} %bitcast.90), channel_id=1, replica_groups=mesh['x'=4,'core'=2,'y'=4,'za'=4,'zb'=2,'zc'=4] {'y'}, dimensions={0} | all-to-all | bytes 2097152 | tf_op jit(solution)/shard_map/all_to_all | solution.py:17
  144.5 0.2 fusion.6
  144.7 0.7 pad_maximum_fusion.1
  145.5 3.4 %all-to-all-start.6 = ((bf16[4,128,256]{2,1,0:T(8,128)(2,1)}), bf16[4,128,256]{2,1,0:T(8,128)(2,1)S(1)}, u32[]{:S(2)}, u32[]{:S(2)}) async-start(bf16[4,128,256]{2,1,0:T(8,128)(2,1)} %pad_maximum_fusion.1), calls=%async_computation.6 | async-start | bytes 524288 | tf_op jit(solution)/shard_map/all_to_all | solution.py:17
  148.9 1.1 convolution_convert_fusion.2
  150.0 0.0 copy-start.3
  150.0 7.5 %all-to-all-done.6 = bf16[4,128,256]{2,1,0:T(8,128)(2,1)S(1)} async-done(((bf16[4,128,256]{2,1,0:T(8,128)(2,1)}), bf16[4,128,256]{2,1,0:T(8,128)(2,1)S(1)}, u32[]{:S(2)}, u32[]{:S(2)}) %all-to-all-start.6) | async-done | bytes 262176 | tf_op jit(solution)/shard_map/all_to_all | solution.py:17
  157.5 0.6 add.148
  158.2 14.6 %all-to-all-start.7 = ((bf16[32,4,256]{2,1,0:T(4,128)(2,1)}), bf16[32,4,256]{2,1,0:T(4,128)(2,1)S(1)}, u32[]{:S(2)}, u32[]{:S(2)}) async-start(bf16[32,4,256]{2,1,0:T(4,128)(2,1)} %add.148), calls=%async_computation.7 | async-start | bytes 131072 | tf_op jit(solution)/shard_map/all_to_all | solution.py:17
  172.8 1.1 convolution_convert_fusion.3
  173.9 0.0 copy-done.3
  173.9 0.0 copy-done.4
  173.9 1.2 convolution_convert_fusion.1
  175.1 22.8 %all-to-all-done.7 = bf16[32,4,256]{2,1,0:T(4,128)(2,1)S(1)} async-done(((bf16[32,4,256]{2,1,0:T(4,128)(2,1)}), bf16[32,4,256]{2,1,0:T(4,128)(2,1)S(1)}, u32[]{:S(2)}, u32[]{:S(2)}) %all-to-all-start.7) | async-done | bytes 65568 | tf_op jit(solution)/shard_map/all_to_all | solution.py:17
  197.9 0.6 add_convert_fusion.4
  (17 shorter events, 0.4 us)
Async XLA Ops:
  2.1 60.2 %all-to-all-start = ((bf16[32,16,128]{2,1,0:T(8,128)(2,1)}), bf16[32,16,128]{2,1,0:T(8,128)(2,1)S(1)}, u32[]{:S(2)}, u32[]{:S(2)}) async-start(bf16[32,16,128]{2,1,0:T(8,128)(2,1)} %bitcast.2), calls=%async_computation | async-start | bytes 262144 | tf_op jit(solution)/shard_map/all_to_all | solution.py:17
  30.8 7.8 %copy-start = (bf16[1024,172]{0,1:T(8,128)(2,1)S(1)}, bf16[1024,172]{0,1:T(8,128)(2,1)}, u32[]{:S(2)}) copy-start(bf16[1024,172]{0,1:T(8,128)(2,1)} %param.12) | copy-start | bytes 1056772
  30.8 7.8 %copy-start.1 = (bf16[1024,172]{0,1:T(8,128)(2,1)S(1)}, bf16[1024,172]{0,1:T(8,128)(2,1)}, u32[]{:S(2)}) copy-start(bf16[1024,172]{0,1:T(8,128)(2,1)} %param.11) | copy-start | bytes 1056772
  32.8 3.3 %collective-permute-start = (f32[176,256]{1,0:T(8,128)S(1)}, f32[176,256]{1,0:T(8,128)S(1)}, u32[]{:S(2)}, u32[]{:S(2)}) collective-permute-start(f32[176,256]{1,0:T(8,128)S(1)} %constant_dynamic-slice_fusion.1), channel_id=1, source_target_pairs={{0,128},{128,0},{1,129},{129,1},{2,130},{130,2},{3,131},{131,3},{4... | collective-permute-start | bytes 540680 | tf_op jit(solution)/shard_map/ppermute | solution.py:76
  36.1 11.9 %copy-start.2 = (s32[512]{0:T(512)S(1)}, s32[512]{0:T(512)}, u32[]{:S(2)}) copy-start(s32[512]{0:T(512)} %param.8) | copy-start | bytes 6148
  36.2 8.5 %collective-permute-start.1 = (f32[176,256]{1,0:T(8,128)S(1)}, f32[176,256]{1,0:T(8,128)S(1)}, u32[]{:S(2)}, u32[]{:S(2)}) collective-permute-start(f32[176,256]{1,0:T(8,128)S(1)} %dynamic-slice_add_fusion), channel_id=1, source_target_pairs={{0,256},{256,0},{512,768},{768,512},{1,257},{257,1},{513,769},{769... | collective-permute-start | bytes 540680 | tf_op jit(solution)/shard_map/ppermute | solution.py:80
  44.7 7.7 %collective-permute-start.2 = (f32[176,256]{1,0:T(8,128)S(1)}, f32[176,256]{1,0:T(8,128)S(1)}, u32[]{:S(2)}, u32[]{:S(2)}) collective-permute-start(f32[176,256]{1,0:T(8,128)S(1)} %add.130), channel_id=1, source_target_pairs={{0,768},{768,0},{256,512},{512,256},{1,769},{769,1},{257,513},{513... | collective-permute-start | bytes 540680 | tf_op jit(solution)/shard_map/ppermute | solution.py:81
  104.5 3.6 %collective-permute-start.3 = (f32[352,256]{1,0:T(8,128)S(1)}, f32[352,256]{1,0:T(8,128)S(1)}, u32[]{:S(2)}, u32[]{:S(2)}) collective-permute-start(f32[352,256]{1,0:T(8,128)S(1)} %constant_dynamic-slice_fusion), channel_id=1, source_target_pairs={{0,128},{128,0},{1,129},{129,1},{2,130},{130,2},{3,131},{131,3},{4... | collective-permute-start | bytes 1081352 | tf_op jit(solution)/shard_map/ppermute | solution.py:76
  145.5 12.0 %all-to-all-start.6 = ((bf16[4,128,256]{2,1,0:T(8,128)(2,1)}), bf16[4,128,256]{2,1,0:T(8,128)(2,1)S(1)}, u32[]{:S(2)}, u32[]{:S(2)}) async-start(bf16[4,128,256]{2,1,0:T(8,128)(2,1)} %pad_maximum_fusion.1), calls=%async_computation.6 | async-start | bytes 524288 | tf_op jit(solution)/shard_map/all_to_all | solution.py:17
  150.0 23.9 %copy-start.3 = (bf16[512,1024]{1,0:T(8,128)(2,1)S(1)}, bf16[512,1024]{1,0:T(8,128)(2,1)}, u32[]{:S(2)}) copy-start(bf16[512,1024]{1,0:T(8,128)(2,1)} %param.10) | copy-start | bytes 3145732
  150.0 23.9 %copy-start.4 = (f32[512]{0:T(512)S(1)}, f32[512]{0:T(512)}, u32[]{:S(2)}) copy-start(f32[512]{0:T(512)} %param.9) | copy-start | bytes 6148
  158.2 39.7 %all-to-all-start.7 = ((bf16[32,4,256]{2,1,0:T(4,128)(2,1)}), bf16[32,4,256]{2,1,0:T(4,128)(2,1)S(1)}, u32[]{:S(2)}, u32[]{:S(2)}) async-start(bf16[32,4,256]{2,1,0:T(4,128)(2,1)} %add.148), calls=%async_computation.7 | async-start | bytes 131072 | tf_op jit(solution)/shard_map/all_to_all | solution.py:17

commit v4 on v2

--- a/solution.py
+++ b/solution.py
@@ -6,18 +6,27 @@
 
 BF = jnp.bfloat16
 F32 = jnp.float32
+NEAR = 4
 
 
 def dot(a, b, i, j):
     return lax.dot_general(a, b, (((i,), (j,)), ((), ())), preferred_element_type=F32)
 
 
-def exchange(x, axis):
-    return lax.all_to_all(x, axis, 0, 0, tiled=True)
+def exchange(x, axis, groups=None):
+    return lax.all_to_all(x, axis, 0, 0, tiled=True, axis_index_groups=groups)
 
 
-def to_all(x, axis, count):
-    return exchange(jnp.broadcast_to(x[None], (count,) + x.shape), axis)
+def to_all(x, axis, count, groups=None):
+    return exchange(jnp.broadcast_to(x[None], (count,) + x.shape), axis, groups)
+
+
+def near(nz):
+    return [list(range(i, i + NEAR)) for i in range(0, nz, NEAR)]
+
+
+def ring(nz):
+    return [[(i + nz // 2) % nz for i in range(nz)]]
 
 
 def cut_lanes(x, count):
@@ -37,23 +46,25 @@
 
 
 def all_tokens_of_y(tokens):
-    nh, nl = lax.axis_size("zh"), lax.axis_size("zl")
+    nz = lax.axis_size("z")
     here, width = tokens.shape
-    cut = cut_lanes(tokens, nl)
-    cut = jnp.broadcast_to(cut[None], (nh,) + cut.shape).reshape(nh * nl, here, width // nl)
-    return exchange(cut, ("zh", "zl")).reshape(nh * nl * here, width // nl)
+    cut = cut_lanes(tokens, NEAR)
+    cut = jnp.broadcast_to(cut[None], (nz // NEAR,) + cut.shape).reshape(nz, here, width // NEAR)
+    return exchange(cut, "z", ring(nz)).reshape(nz * here, width // NEAR)
 
 
 def gather_routed(held, route_index):
-    ny, nl = lax.axis_size("y"), lax.axis_size("zl")
-    count, quarter = held.shape
+    ny, nz = lax.axis_size("y"), lax.axis_size("z")
+    count, part = held.shape
     rows = route_index.shape[0]
     place = route_index - lax.axis_index("y") * count
+    held_at = jnp.where(place < count // 2, place + count // 2, place - count // 2)
+    place = jnp.where((place >= 0) & (place < count), held_at, -1)
     pick = (place[:, None] == lax.broadcasted_iota(jnp.int32, (rows, count), 1)).astype(BF)
     filled = jnp.dot(pick, held, preferred_element_type=F32).astype(BF)
-    got = add_up(exchange(filled.reshape(ny, rows // ny, quarter), "y")).astype(BF)
-    got = join_lanes(to_all(got, "zl", nl))
-    return to_all(got, "y", ny).reshape(rows, nl * quarter)
+    got = add_up(exchange(filled.reshape(ny, rows // ny, part), "y")).astype(BF)
+    got = join_lanes(to_all(got, "z", NEAR, near(nz)))
+    return to_all(got, "y", ny).reshape(rows, NEAR * part)
 
 
 def activate(gate, up, back):
@@ -80,14 +91,15 @@
 
 def scatter_rows(total, out_grad):
     rows, width = total.shape
-    ny, nh, nl = lax.axis_size("y"), lax.axis_size("zh"), lax.axis_size("zl")
-    slots, quarter = rows // ny, width // nl
-    each = slots // (nh * nl)
+    ny, nz = lax.axis_size("y"), lax.axis_size("z")
+    slots, quarter = rows // ny, width // NEAR
+    each = slots // nz
     part = add_up(exchange(total.reshape(ny, slots, width), "y")).astype(BF)
-    part = add_up(exchange(cut_lanes(part, nl), "zl")).astype(BF)
-    part = exchange(part.reshape(nh * nl, each, quarter), ("zh", "zl"))
-    part = join_lanes(add_up(part.reshape(nh, nl, each, quarter)))
-    first = lax.axis_index(("y", "zh", "zl")) * each
+    part = add_up(exchange(cut_lanes(part, NEAR), "z", near(nz))).astype(BF)
+    part = jnp.concatenate([part[slots // 2 :], part[: slots // 2]])
+    part = exchange(part.reshape(nz, each, quarter), "z", ring(nz))
+    part = join_lanes(add_up(part.reshape(nz // NEAR, NEAR, each, quarter)))
+    first = lax.axis_index(("y", "z")) * each
     mine = lax.dynamic_slice_in_dim(out_grad, first, each, 0)
     return (mine.astype(F32) + part).astype(BF)
 
@@ -115,8 +127,8 @@
 
 def solution(mesh):
     rows, cols = mesh.devices.shape
-    fine = Mesh(mesh.devices.reshape(rows // 2, 2, 4, cols // 16, 4), ("x", "core", "y", "zh", "zl"))
-    row, col = ("x", "core"), ("y", "zh", "zl")
+    fine = Mesh(mesh.devices.reshape(rows // 2, 2, 4, cols // 4), ("x", "core", "y", "z"))
+    row, col = ("x", "core"), ("y", "z")
     placed = (
         P(col, row),
         P(),

time: 193 us -> 181 us (0.938)
  waiting for transfers between devices: 63.9 us -> 24.8 us
  starting transfers between devices: 47 us -> 71.8 us
    all_to_all x3, waiting for transfers between devices: 50.7 us -> 11.6 us  [exchange(): return lax.all_to_all(x, axis, 0, 0, tiled=True, axis_index_groups=groups)]
    all_to_all x3, starting transfers between devices: 37.3 us -> 62.1 us  [exchange(): return lax.all_to_all(x, axis, 0, 0, tiled=True, axis_index_groups=groups)]
where the time goes in v4:
time: 181 us; the launch traced here: 180 us
  starting transfers between devices  71.8 us (40%)
  blocking collectives  71 us (39%)
  waiting for transfers between devices  24.8 us (14%)
  matrix products  6.96 us (4%)
  local copies, waits for them, and re-layouts  2.46 us (1%)
  other arithmetic  2.09 us (1%)
    all_to_all x5, blocking collectives, exchange(): return lax.all_to_all(x, axis, 0, 0, tiled=True, axis_index_groups=groups)  68.8 us
    all_to_all x3, starting transfers between devices, exchange(): return lax.all_to_all(x, axis, 0, 0, tiled=True, axis_index_groups=groups)  62.1 us
    all_to_all x3, waiting for transfers between devices, exchange(): return lax.all_to_all(x, axis, 0, 0, tiled=True, axis_index_groups=groups)  11.6 us
    dot_general x6, matrix products, dot(): lax.dot_general(a, b, (((i,), (j,)), ((), ())), preferred_element_type=F32)  6.6 us
    ppermute x1, waiting for transfers between devices, sum_by_pairs(): part = part + lax.ppermute(part, 'x', [(0, 1), (1, 0), (2, 3), (3, 2)])  5.95 us
    ppermute x1, waiting for transfers between devices, sum_by_pairs(): return part + lax.ppermute(part, 'x', [(0, 3), (3, 0), (1, 2), (2, 1)])  4.23 us
    ppermute x2, starting transfers between devices, chip_sum(): return keep + lax.ppermute(give, 'core', [(0, 1), (1, 0)])  3.84 us
  transfers between devices with their start and end apart: 7, of which 7 were waited for; matrix products, arithmetic and copies ran while one was open for 3% of the time, Pallas kernels for 0%

profile of v4, /device:TPU:2, one launch (start us, length us, event | category | flops | bytes accessed | tf_op | source)
XLA Modules:
  0.0 180.1 jit_solution(16539701153684264462)
XLA Ops:
  0.6 0.8 slice_bitcast_fusion.21
  1.4 0.7 broadcast_in_dim.14
  2.1 35.9 %all-to-all-start = ((bf16[32,16,256]{2,1,0:T(8,128)(2,1)}), bf16[32,16,256]{2,1,0:T(8,128)(2,1)S(1)}, u32[]{:S(2)}, u32[]{:S(2)}) async-start(bf16[32,16,256]{2,1,0:T(8,128)(2,1)} %bitcast.4), calls=%async_computation | async-start | bytes 524288 | tf_op jit(solution)/shard_map/all_to_all | solution.py:17
  38.0 0.0 copy-start
  38.0 0.0 copy-start.1
  38.0 1.9 %fusion.4 = f32[176,512]{1,0:T(8,128)S(1)} fusion(bf16[512,1024]{1,0:T(8,128)(2,1)} %param.10, f32[512]{0:T(512)} %param.9, bf16[172,1024]{1,0:T(8,128)(2,1)} %param.13), kind=kOutput, calls=%fused_computation.14 | convolution fusion | flops 186122240 | bytes 1763328 | tf_op jit(solution)/shard_map/dot_general | solution.py:13
  40.0 1.9 %collective-permute-start = (f32[176,256]{1,0:T(8,128)S(1)}, f32[176,256]{1,0:T(8,128)S(1)}, u32[]{:S(2)}, u32[]{:S(2)}) collective-permute-start(f32[176,256]{1,0:T(8,128)S(1)} %constant_dynamic-slice_fusion.1), channel_id=1, source_target_pairs={{0,128},{128,0},{1,129},{129,1},{2,130},{130,2},{3,131},{131,3},{4... | collective-permute-start | bytes 540680 | tf_op jit(solution)/shard_map/ppermute | solution.py:84
  41.9 1.4 collective-permute-done
  43.3 0.0 copy-start.2
  43.4 2.4 %collective-permute-start.1 = (f32[176,256]{1,0:T(8,128)S(1)}, f32[176,256]{1,0:T(8,128)S(1)}, u32[]{:S(2)}, u32[]{:S(2)}) collective-permute-start(f32[176,256]{1,0:T(8,128)S(1)} %dynamic-slice_add_fusion), channel_id=1, source_target_pairs={{0,256},{256,0},{512,768},{768,512},{1,257},{257,1},{513,769},{769... | collective-permute-start | bytes 540680 | tf_op jit(solution)/shard_map/ppermute | solution.py:88
  45.8 0.0 copy-done
  45.8 0.0 copy-done.1
  45.8 0.1 fusion.2
  45.9 6.0 %collective-permute-done.1 = f32[176,256]{1,0:T(8,128)S(1)} collective-permute-done((f32[176,256]{1,0:T(8,128)S(1)}, f32[176,256]{1,0:T(8,128)S(1)}, u32[]{:S(2)}, u32[]{:S(2)}) %collective-permute-start.1) | collective-permute-done | bytes 180256 | tf_op jit(solution)/shard_map/ppermute | solution.py:88
  51.9 3.4 %collective-permute-start.2 = (f32[176,256]{1,0:T(8,128)S(1)}, f32[176,256]{1,0:T(8,128)S(1)}, u32[]{:S(2)}, u32[]{:S(2)}) collective-permute-start(f32[176,256]{1,0:T(8,128)S(1)} %add.121), channel_id=1, source_target_pairs={{0,768},{768,0},{256,512},{512,256},{1,769},{769,1},{257,513},{513... | collective-permute-start | bytes 540680 | tf_op jit(solution)/shard_map/ppermute | solution.py:89
  55.3 0.0 copy-done.2
  55.3 4.2 %collective-permute-done.2 = f32[176,256]{1,0:T(8,128)S(1)} collective-permute-done((f32[176,256]{1,0:T(8,128)S(1)}, f32[176,256]{1,0:T(8,128)S(1)}, u32[]{:S(2)}, u32[]{:S(2)}) %collective-permute-start.2) | collective-permute-done | bytes 180256 | tf_op jit(solution)/shard_map/ppermute | solution.py:89
  59.6 1.4 all-to-all-done
  61.0 0.4 convolution_convert_fusion.4
  61.4 10.9 %all_to_all.40 = bf16[4,128,256]{2,1,0:T(8,128)(2,1)S(1)} all-to-all(bf16[4,128,256]{2,1,0:T(8,128)(2,1)S(1)} %bitcast.100), channel_id=1, replica_groups=mesh['x'=4,'core'=2,'y'=4,'z'=32] {'y'}, dimensions={0} | all-to-all | bytes 524288 | tf_op jit(solution)/shard_map/all_to_all | solution.py:17
  72.4 11.0 %all_to_all.41 = bf16[4,128,256]{2,1,0:T(8,128)(2,1)S(1)} all-to-all(bf16[4,128,256]{2,1,0:T(8,128)(2,1)S(1)} %broadcast_in_dim.17), channel_id=1, replica_groups={{0,1,2,3},{4,5,6,7},{8,9,10,11},{12,13,14,15},{16,17,18,19},{20,21,22,2..., dimensions={0} | all-to-all | bytes 524288 | tf_op jit(solution)/shard_map/all_to_all | solution.py:17
  83.5 0.1 broadcast_in_dim.18
  83.6 13.7 %all_to_all.42 = bf16[4,128,1024]{2,1,0:T(8,128)(2,1)S(1)} all-to-all(bf16[4,128,1024]{2,1,0:T(8,128)(2,1)S(1)} %broadcast_in_dim.18), channel_id=1, replica_groups=mesh['x'=4,'core'=2,'y'=4,'z'=32] {'y'}, dimensions={0} | all-to-all | bytes 2097152 | tf_op jit(solution)/shard_map/all_to_all | solution.py:17
  97.3 0.6 fusion.14
  97.9 1.9 %collective-permute-start.3 = (f32[352,256]{1,0:T(8,128)S(1)}, f32[352,256]{1,0:T(8,128)S(1)}, u32[]{:S(2)}, u32[]{:S(2)}) collective-permute-start(f32[352,256]{1,0:T(8,128)S(1)} %constant_dynamic-slice_fusion), channel_id=1, source_target_pairs={{0,128},{128,0},{1,129},{129,1},{2,130},{130,2},{3,131},{131,3},{4... | collective-permute-start | bytes 1081352 | tf_op jit(solution)/shard_map/ppermute | solution.py:84
  99.8 1.6 collective-permute-done.3
  101.5 0.1 add_convert_fusion.1
  101.6 15.1 %all_to_all.43 = bf16[4,352,256]{2,1,0:T(8,128)(2,1)S(1)} all-to-all(bf16[4,352,256]{2,1,0:T(8,128)(2,1)S(1)} %broadcast_in_dim.19), channel_id=1, replica_groups=mesh['x'=4,'core'=2,'y'=4,'z'=32] {'x'}, dimensions={0} | all-to-all | bytes 1441792 | tf_op jit(solution)/shard_map/all_to_all | solution.py:17
  116.7 0.1 convert_add_fusion
  116.7 0.1 fusion.10
  116.9 2.2 %all_gather.3 = bf16[3,176,512]{2,1,0:T(8,128)(2,1)S(1)} all-gather(bf16[3,176,256]{2,1,0:T(8,128)(2,1)S(1)} %pad_maximum_fusion), channel_id=1, replica_groups=mesh['x'=4,'core'=2,'y'=4,'z'=32] {'core'}, dimensions={2}, use_global_device_ids=true | all-gather | bytes 811008 | tf_op jit(solution)/shard_map/all_gather | solution.py:119
  119.1 0.7 convolution_convert_fusion
  119.9 18.1 %all_to_all.44 = bf16[4,128,1024]{2,1,0:T(8,128)(2,1)S(1)} all-to-all(bf16[4,128,1024]{2,1,0:T(8,128)(2,1)S(1)} %bitcast.95), channel_id=1, replica_groups=mesh['x'=4,'core'=2,'y'=4,'z'=32] {'y'}, dimensions={0} | all-to-all | bytes 2097152 | tf_op jit(solution)/shard_map/all_to_all | solution.py:17
  138.0 0.2 fusion.6
  138.2 0.7 pad_maximum_fusion.2
  138.9 3.4 %all-to-all-start.6 = ((bf16[4,128,256]{2,1,0:T(8,128)(2,1)}), bf16[4,128,256]{2,1,0:T(8,128)(2,1)S(1)}, u32[]{:S(2)}, u32[]{:S(2)}) async-start(bf16[4,128,256]{2,1,0:T(8,128)(2,1)} %pad_maximum_fusion.2), calls=%async_computation.6 | async-start | bytes 524288 | tf_op jit(solution)/shard_map/all_to_all | solution.py:17
  142.3 1.1 convolution_convert_fusion.2
  143.4 7.5 %all-to-all-done.6 = bf16[4,128,256]{2,1,0:T(8,128)(2,1)S(1)} async-done(((bf16[4,128,256]{2,1,0:T(8,128)(2,1)}), bf16[4,128,256]{2,1,0:T(8,128)(2,1)S(1)}, u32[]{:S(2)}, u32[]{:S(2)}) %all-to-all-start.6) | async-done | bytes 262176 | tf_op jit(solution)/shard_map/all_to_all | solution.py:17
  150.9 0.0 copy-start.3
  151.0 0.0 copy-start.4
  151.0 0.6 reshape.84
  151.6 22.8 %all-to-all-start.7 = ((bf16[32,4,256]{2,1,0:T(4,128)(2,1)}), bf16[32,4,256]{2,1,0:T(4,128)(2,1)S(1)}, u32[]{:S(2)}, u32[]{:S(2)}) async-start(bf16[32,4,256]{2,1,0:T(4,128)(2,1)} %reshape.84), calls=%async_computation.7 | async-start | bytes 131072 | tf_op jit(solution)/shard_map/all_to_all | solution.py:17
  174.5 1.1 convolution_convert_fusion.3
  175.6 0.0 copy-done.3
  175.6 0.0 copy-done.4
  175.6 1.2 convolution_convert_fusion.1
  176.8 2.7 %all-to-all-done.7 = bf16[32,4,256]{2,1,0:T(4,128)(2,1)S(1)} async-done(((bf16[32,4,256]{2,1,0:T(4,128)(2,1)}), bf16[32,4,256]{2,1,0:T(4,128)(2,1)S(1)}, u32[]{:S(2)}, u32[]{:S(2)}) %all-to-all-start.7) | async-done | bytes 65568 | tf_op jit(solution)/shard_map/all_to_all | solution.py:17
  179.5 0.6 fusion.12
  (20 shorter events, 0.4 us)
Async XLA Ops:
  2.1 58.9 %all-to-all-start = ((bf16[32,16,256]{2,1,0:T(8,128)(2,1)}), bf16[32,16,256]{2,1,0:T(8,128)(2,1)S(1)}, u32[]{:S(2)}, u32[]{:S(2)}) async-start(bf16[32,16,256]{2,1,0:T(8,128)(2,1)} %bitcast.4), calls=%async_computation | async-start | bytes 524288 | tf_op jit(solution)/shard_map/all_to_all | solution.py:17
  38.0 7.8 %copy-start = (bf16[1024,172]{0,1:T(8,128)(2,1)S(1)}, bf16[1024,172]{0,1:T(8,128)(2,1)}, u32[]{:S(2)}) copy-start(bf16[1024,172]{0,1:T(8,128)(2,1)} %param.12) | copy-start | bytes 1056772
  38.0 7.8 %copy-start.1 = (bf16[1024,172]{0,1:T(8,128)(2,1)S(1)}, bf16[1024,172]{0,1:T(8,128)(2,1)}, u32[]{:S(2)}) copy-start(bf16[1024,172]{0,1:T(8,128)(2,1)} %param.11) | copy-start | bytes 1056772
  40.0 3.3 %collective-permute-start = (f32[176,256]{1,0:T(8,128)S(1)}, f32[176,256]{1,0:T(8,128)S(1)}, u32[]{:S(2)}, u32[]{:S(2)}) collective-permute-start(f32[176,256]{1,0:T(8,128)S(1)} %constant_dynamic-slice_fusion.1), channel_id=1, source_target_pairs={{0,128},{128,0},{1,129},{129,1},{2,130},{130,2},{3,131},{131,3},{4... | collective-permute-start | bytes 540680 | tf_op jit(solution)/shard_map/ppermute | solution.py:84
  43.3 11.9 %copy-start.2 = (s32[512]{0:T(512)S(1)}, s32[512]{0:T(512)}, u32[]{:S(2)}) copy-start(s32[512]{0:T(512)} %param.8) | copy-start | bytes 6148
  43.4 8.5 %collective-permute-start.1 = (f32[176,256]{1,0:T(8,128)S(1)}, f32[176,256]{1,0:T(8,128)S(1)}, u32[]{:S(2)}, u32[]{:S(2)}) collective-permute-start(f32[176,256]{1,0:T(8,128)S(1)} %dynamic-slice_add_fusion), channel_id=1, source_target_pairs={{0,256},{256,0},{512,768},{768,512},{1,257},{257,1},{513,769},{769... | collective-permute-start | bytes 540680 | tf_op jit(solution)/shard_map/ppermute | solution.py:88
  51.9 7.7 %collective-permute-start.2 = (f32[176,256]{1,0:T(8,128)S(1)}, f32[176,256]{1,0:T(8,128)S(1)}, u32[]{:S(2)}, u32[]{:S(2)}) collective-permute-start(f32[176,256]{1,0:T(8,128)S(1)} %add.121), channel_id=1, source_target_pairs={{0,768},{768,0},{256,512},{512,256},{1,769},{769,1},{257,513},{513... | collective-permute-start | bytes 540680 | tf_op jit(solution)/shard_map/ppermute | solution.py:89
  97.9 3.6 %collective-permute-start.3 = (f32[352,256]{1,0:T(8,128)S(1)}, f32[352,256]{1,0:T(8,128)S(1)}, u32[]{:S(2)}, u32[]{:S(2)}) collective-permute-start(f32[352,256]{1,0:T(8,128)S(1)} %constant_dynamic-slice_fusion), channel_id=1, source_target_pairs={{0,128},{128,0},{1,129},{129,1},{2,130},{130,2},{3,131},{131,3},{4... | collective-permute-start | bytes 1081352 | tf_op jit(solution)/shard_map/ppermute | solution.py:84
  138.9 12.0 %all-to-all-start.6 = ((bf16[4,128,256]{2,1,0:T(8,128)(2,1)}), bf16[4,128,256]{2,1,0:T(8,128)(2,1)S(1)}, u32[]{:S(2)}, u32[]{:S(2)}) async-start(bf16[4,128,256]{2,1,0:T(8,128)(2,1)} %pad_maximum_fusion.2), calls=%async_computation.6 | async-start | bytes 524288 | tf_op jit(solution)/shard_map/all_to_all | solution.py:17
  150.9 24.6 %copy-start.3 = (bf16[512,1024]{1,0:T(8,128)(2,1)S(1)}, bf16[512,1024]{1,0:T(8,128)(2,1)}, u32[]{:S(2)}) copy-start(bf16[512,1024]{1,0:T(8,128)(2,1)} %param.10) | copy-start | bytes 3145732
  151.0 24.6 %copy-start.4 = (f32[512]{0:T(512)S(1)}, f32[512]{0:T(512)}, u32[]{:S(2)}) copy-start(f32[512]{0:T(512)} %param.9) | copy-start | bytes 6148
  151.6 27.8 %all-to-all-start.7 = ((bf16[32,4,256]{2,1,0:T(4,128)(2,1)}), bf16[32,4,256]{2,1,0:T(4,128)(2,1)S(1)}, u32[]{:S(2)}, u32[]{:S(2)}) async-start(bf16[32,4,256]{2,1,0:T(4,128)(2,1)} %reshape.84), calls=%async_computation.7 | async-start | bytes 131072 | tf_op jit(solution)/shard_map/all_to_all | solution.py:17

commit v5 on v4

--- a/solution.py
+++ b/solution.py
@@ -6,6 +6,7 @@
 
 BF = jnp.bfloat16
 F32 = jnp.float32
+PARTS = 8
 NEAR = 4
 
 
@@ -21,21 +22,28 @@
     return exchange(jnp.broadcast_to(x[None], (count,) + x.shape), axis, groups)
 
 
-def near(nz):
-    return [list(range(i, i + NEAR)) for i in range(0, nz, NEAR)]
+def near(nz, count):
+    order = [(i + count // 2) % count for i in range(count)]
+    return [[i + j for j in order] for i in range(0, nz, count)]
 
 
-def ring(nz):
-    return [[(i + nz // 2) % nz for i in range(nz)]]
+def ring_start(nz, count):
+    return 5 * nz // 8 // count * count + count // 2
+
+
+def ring(nz, count):
+    return [[(i + ring_start(nz, count)) % nz for i in range(nz)]]
 
 
 def cut_lanes(x, count):
-    width = x.shape[1] // count
-    return jnp.stack([x[:, i * width : (i + 1) * width] for i in range(count)])
+    rows, width = x.shape
+    part = width // count
+    return x.reshape(rows // 8, 8, count, part).transpose(2, 0, 1, 3).reshape(count, rows, part)
 
 
 def join_lanes(x):
-    return jnp.concatenate([x[i] for i in range(x.shape[0])], axis=1)
+    count, rows, part = x.shape
+    return x.reshape(count, rows // 8, 8, part).transpose(1, 2, 0, 3).reshape(rows, count * part)
 
 
 def add_up(x):
@@ -48,9 +56,9 @@
 def all_tokens_of_y(tokens):
     nz = lax.axis_size("z")
     here, width = tokens.shape
-    cut = cut_lanes(tokens, NEAR)
-    cut = jnp.broadcast_to(cut[None], (nz // NEAR,) + cut.shape).reshape(nz, here, width // NEAR)
-    return exchange(cut, "z", ring(nz)).reshape(nz * here, width // NEAR)
+    cut = cut_lanes(tokens, PARTS)
+    cut = jnp.broadcast_to(cut[None], (nz // PARTS,) + cut.shape).reshape(nz, here, width // PARTS)
+    return exchange(cut, "z", ring(nz, PARTS)).reshape(nz * here, width // PARTS)
 
 
 def gather_routed(held, route_index):
@@ -58,13 +66,14 @@
     count, part = held.shape
     rows = route_index.shape[0]
     place = route_index - lax.axis_index("y") * count
-    held_at = jnp.where(place < count // 2, place + count // 2, place - count // 2)
+    first = ring_start(nz, PARTS) * (count // nz)
+    held_at = jnp.where(place < first, place + (count - first), place - first)
     place = jnp.where((place >= 0) & (place < count), held_at, -1)
     pick = (place[:, None] == lax.broadcasted_iota(jnp.int32, (rows, count), 1)).astype(BF)
     filled = jnp.dot(pick, held, preferred_element_type=F32).astype(BF)
     got = add_up(exchange(filled.reshape(ny, rows // ny, part), "y")).astype(BF)
-    got = join_lanes(to_all(got, "z", NEAR, near(nz)))
-    return to_all(got, "y", ny).reshape(rows, NEAR * part)
+    got = join_lanes(to_all(got, "z", PARTS, near(nz, PARTS)))
+    return to_all(got, "y", ny).reshape(rows, PARTS * part)
 
 
 def activate(gate, up, back):
@@ -95,10 +104,12 @@
     slots, quarter = rows // ny, width // NEAR
     each = slots // nz
     part = add_up(exchange(total.reshape(ny, slots, width), "y")).astype(BF)
-    part = add_up(exchange(cut_lanes(part, NEAR), "z", near(nz))).astype(BF)
-    part = jnp.concatenate([part[slots // 2 :], part[: slots // 2]])
-    part = exchange(part.reshape(nz, each, quarter), "z", ring(nz))
-    part = join_lanes(add_up(part.reshape(nz // NEAR, NEAR, each, quarter)))
+    part = jnp.stack([part[:, i * quarter : (i + 1) * quarter] for i in range(NEAR)])
+    part = exchange(part, "z", near(nz, NEAR))
+    turn = ring_start(nz, NEAR) * each
+    part = jnp.concatenate([add_up(part[:, turn:]), add_up(part[:, :turn])]).astype(BF)
+    part = exchange(part.reshape(nz, each, quarter), "z", ring(nz, NEAR))
+    part = add_up(part.reshape(nz // NEAR, NEAR, each, quarter)).transpose(1, 0, 2).reshape(each, width)
     first = lax.axis_index(("y", "z")) * each
     mine = lax.dynamic_slice_in_dim(out_grad, first, each, 0)
     return (mine.astype(F32) + part).astype(BF)

time: 181 us -> 186 us (1.028)
  blocking collectives: 71 us -> 76.3 us
  starting transfers between devices: 71.8 us -> 69.1 us
  waiting for transfers between devices: 24.8 us -> 27.4 us
    all_to_all x5, blocking collectives: 68.8 us -> 74.1 us  [exchange(): return lax.all_to_all(x, axis, 0, 0, tiled=True, axis_index_groups=groups)]
    all_to_all x3, starting transfers between devices: 62.1 us -> 59.4 us  [exchange(): return lax.all_to_all(x, axis, 0, 0, tiled=True, axis_index_groups=groups)]
    all_to_all x3, waiting for transfers between devices: 11.6 us -> 14.2 us  [exchange(): return lax.all_to_all(x, axis, 0, 0, tiled=True, axis_index_groups=groups)]
  transfers between devices with their start and end apart: 7 -> 7, of which waited for: 7 -> 6; matrix products, arithmetic and copies ran while one was open for 3% -> 3% of each run, Pallas kernels for 0% -> 0%
where the time goes in v5:
time: 186 us; the launch traced here: 185 us
  blocking collectives  76.3 us (41%)
  starting transfers between devices  69.1 us (37%)
  waiting for transfers between devices  27.4 us (15%)
  matrix products  6.96 us (4%)
  local copies, waits for them, and re-layouts  2.64 us (1%)
  other arithmetic  2.06 us (1%)
    all_to_all x5, blocking collectives, exchange(): return lax.all_to_all(x, axis, 0, 0, tiled=True, axis_index_groups=groups)  74.1 us
    all_to_all x3, starting transfers between devices, exchange(): return lax.all_to_all(x, axis, 0, 0, tiled=True, axis_index_groups=groups)  59.4 us
    all_to_all x3, waiting for transfers between devices, exchange(): return lax.all_to_all(x, axis, 0, 0, tiled=True, axis_index_groups=groups)  14.2 us
    dot_general x6, matrix products, dot(): lax.dot_general(a, b, (((i,), (j,)), ((), ())), preferred_element_type=F32)  6.6 us
    ppermute x1, waiting for transfers between devices, sum_by_pairs(): part = part + lax.ppermute(part, 'x', [(0, 1), (1, 0), (2, 3), (3, 2)])  5.96 us
    ppermute x1, waiting for transfers between devices, sum_by_pairs(): return part + lax.ppermute(part, 'x', [(0, 3), (3, 0), (1, 2), (2, 1)])  4.23 us
    ppermute x2, starting transfers between devices, chip_sum(): return keep + lax.ppermute(give, 'core', [(0, 1), (1, 0)])  3.84 us
  transfers between devices with their start and end apart: 7, of which 6 were waited for; matrix products, arithmetic and copies ran while one was open for 3% of the time, Pallas kernels for 0%

profile of v5, /device:TPU:2, one launch (start us, length us, event | category | flops | bytes accessed | tf_op | source)
XLA Modules:
  0.0 185.4 jit_solution(5599907466338435665)
XLA Ops:
  0.6 0.8 copy.25
  1.4 0.7 broadcast_in_dim.35
  2.1 31.1 %all-to-all-start = ((bf16[32,16,128]{2,1,0:T(8,128)(2,1)}), bf16[32,16,128]{2,1,0:T(8,128)(2,1)S(1)}, u32[]{:S(2)}, u32[]{:S(2)}) async-start(bf16[32,16,128]{2,1,0:T(8,128)(2,1)} %bitcast.2), calls=%async_computation | async-start | bytes 262144 | tf_op jit(solution)/shard_map/all_to_all | solution.py:18
  33.2 0.0 copy-start
  33.2 0.0 copy-start.1
  33.2 1.9 %fusion.4 = f32[176,512]{1,0:T(8,128)S(1)} fusion(bf16[512,1024]{1,0:T(8,128)(2,1)} %param.10, f32[512]{0:T(512)} %param.9, bf16[172,1024]{1,0:T(8,128)(2,1)} %param.13), kind=kOutput, calls=%fused_computation.14 | convolution fusion | flops 186122240 | bytes 1763328 | tf_op jit(solution)/shard_map/dot_general | solution.py:14
  35.2 1.9 %collective-permute-start = (f32[176,256]{1,0:T(8,128)S(1)}, f32[176,256]{1,0:T(8,128)S(1)}, u32[]{:S(2)}, u32[]{:S(2)}) collective-permute-start(f32[176,256]{1,0:T(8,128)S(1)} %constant_dynamic-slice_fusion.1), channel_id=1, source_target_pairs={{0,128},{128,0},{1,129},{129,1},{2,130},{130,2},{3,131},{131,3},{4... | collective-permute-start | bytes 540680 | tf_op jit(solution)/shard_map/ppermute | solution.py:93
  37.1 1.4 collective-permute-done
  38.5 0.0 copy-start.2
  38.5 2.4 %collective-permute-start.1 = (f32[176,256]{1,0:T(8,128)S(1)}, f32[176,256]{1,0:T(8,128)S(1)}, u32[]{:S(2)}, u32[]{:S(2)}) collective-permute-start(f32[176,256]{1,0:T(8,128)S(1)} %dynamic-slice_add_fusion), channel_id=1, source_target_pairs={{0,256},{256,0},{512,768},{768,512},{1,257},{257,1},{513,769},{769... | collective-permute-start | bytes 540680 | tf_op jit(solution)/shard_map/ppermute | solution.py:97
  41.0 0.0 copy-done
  41.0 0.0 copy-done.1
  41.0 0.1 fusion.2
  41.0 6.0 %collective-permute-done.1 = f32[176,256]{1,0:T(8,128)S(1)} collective-permute-done((f32[176,256]{1,0:T(8,128)S(1)}, f32[176,256]{1,0:T(8,128)S(1)}, u32[]{:S(2)}, u32[]{:S(2)}) %collective-permute-start.1) | collective-permute-done | bytes 180256 | tf_op jit(solution)/shard_map/ppermute | solution.py:97
  47.0 3.4 %collective-permute-start.2 = (f32[176,256]{1,0:T(8,128)S(1)}, f32[176,256]{1,0:T(8,128)S(1)}, u32[]{:S(2)}, u32[]{:S(2)}) collective-permute-start(f32[176,256]{1,0:T(8,128)S(1)} %add.140), channel_id=1, source_target_pairs={{0,768},{768,0},{256,512},{512,256},{1,769},{769,1},{257,513},{513... | collective-permute-start | bytes 540680 | tf_op jit(solution)/shard_map/ppermute | solution.py:98
  50.4 0.0 copy-done.2
  50.5 4.2 %collective-permute-done.2 = f32[176,256]{1,0:T(8,128)S(1)} collective-permute-done((f32[176,256]{1,0:T(8,128)S(1)}, f32[176,256]{1,0:T(8,128)S(1)}, u32[]{:S(2)}, u32[]{:S(2)}) %collective-permute-start.2) | collective-permute-done | bytes 180256 | tf_op jit(solution)/shard_map/ppermute | solution.py:98
  54.7 0.0 all-to-all-done
  54.7 0.4 convolution_convert_fusion.4
  55.1 10.2 %all_to_all.40 = bf16[4,128,128]{2,1,0:T(8,128)(2,1)S(1)} all-to-all(bf16[4,128,128]{2,1,0:T(8,128)(2,1)S(1)} %bitcast.103), channel_id=1, replica_groups=mesh['x'=4,'core'=2,'y'=4,'z'=32] {'y'}, dimensions={0} | all-to-all | bytes 262144 | tf_op jit(solution)/shard_map/all_to_all | solution.py:18
  65.4 16.4 %all_to_all.41 = bf16[8,128,128]{2,1,0:T(8,128)(2,1)S(1)} all-to-all(bf16[8,128,128]{2,1,0:T(8,128)(2,1)S(1)} %broadcast_in_dim.38), channel_id=1, replica_groups={{4,5,6,7,0,1,2,3},{12,13,14,15,8,9,10,11},{20,21,22,23,16,17,18,19},{28..., dimensions={0} | all-to-all | bytes 524288 | tf_op jit(solution)/shard_map/all_to_all | solution.py:18
  81.8 0.2 copy.24
  82.1 0.1 broadcast_in_dim.40
  82.2 13.3 %all_to_all.42 = bf16[4,128,1024]{2,1,0:T(8,128)(2,1)S(1)} all-to-all(bf16[4,128,1024]{2,1,0:T(8,128)(2,1)S(1)} %broadcast_in_dim.40), channel_id=1, replica_groups=mesh['x'=4,'core'=2,'y'=4,'z'=32] {'y'}, dimensions={0} | all-to-all | bytes 2097152 | tf_op jit(solution)/shard_map/all_to_all | solution.py:18
  95.5 0.6 fusion.15
  96.1 1.9 %collective-permute-start.3 = (f32[352,256]{1,0:T(8,128)S(1)}, f32[352,256]{1,0:T(8,128)S(1)}, u32[]{:S(2)}, u32[]{:S(2)}) collective-permute-start(f32[352,256]{1,0:T(8,128)S(1)} %constant_dynamic-slice_fusion), channel_id=1, source_target_pairs={{0,128},{128,0},{1,129},{129,1},{2,130},{130,2},{3,131},{131,3},{4... | collective-permute-start | bytes 1081352 | tf_op jit(solution)/shard_map/ppermute | solution.py:93
  98.1 1.6 collective-permute-done.3
  99.7 0.1 add_convert_fusion.1
  99.8 16.0 %all_to_all.43 = bf16[4,352,256]{2,1,0:T(8,128)(2,1)S(1)} all-to-all(bf16[4,352,256]{2,1,0:T(8,128)(2,1)S(1)} %broadcast_in_dim.41), channel_id=1, replica_groups=mesh['x'=4,'core'=2,'y'=4,'z'=32] {'x'}, dimensions={0} | all-to-all | bytes 1441792 | tf_op jit(solution)/shard_map/all_to_all | solution.py:18
  115.8 0.1 convert_add_fusion
  115.9 0.1 fusion.10
  116.1 2.2 %all_gather.3 = bf16[3,176,512]{2,1,0:T(8,128)(2,1)S(1)} all-gather(bf16[3,176,256]{2,1,0:T(8,128)(2,1)S(1)} %pad_maximum_fusion), channel_id=1, replica_groups=mesh['x'=4,'core'=2,'y'=4,'z'=32] {'core'}, dimensions={2}, use_global_device_ids=true | all-gather | bytes 811008 | tf_op jit(solution)/shard_map/all_gather | solution.py:130
  118.3 0.7 convolution_convert_fusion
  119.1 18.1 %all_to_all.44 = bf16[4,128,1024]{2,1,0:T(8,128)(2,1)S(1)} all-to-all(bf16[4,128,1024]{2,1,0:T(8,128)(2,1)S(1)} %bitcast.94), channel_id=1, replica_groups=mesh['x'=4,'core'=2,'y'=4,'z'=32] {'y'}, dimensions={0} | all-to-all | bytes 2097152 | tf_op jit(solution)/shard_map/all_to_all | solution.py:18
  137.2 0.2 fusion.6
  137.4 0.7 pad_maximum_fusion.1
  138.1 4.6 %all-to-all-start.6 = ((bf16[4,128,256]{2,1,0:T(8,128)(2,1)}), bf16[4,128,256]{2,1,0:T(8,128)(2,1)S(1)}, u32[]{:S(2)}, u32[]{:S(2)}) async-start(bf16[4,128,256]{2,1,0:T(8,128)(2,1)} %pad_maximum_fusion.1), calls=%async_computation.6 | async-start | bytes 524288 | tf_op jit(solution)/shard_map/all_to_all | solution.py:18
  142.7 1.1 convolution_convert_fusion.2
  143.8 5.0 %all-to-all-done.6 = bf16[4,128,256]{2,1,0:T(8,128)(2,1)S(1)} async-done(((bf16[4,128,256]{2,1,0:T(8,128)(2,1)}), bf16[4,128,256]{2,1,0:T(8,128)(2,1)S(1)}, u32[]{:S(2)}, u32[]{:S(2)}) %all-to-all-start.6) | async-done | bytes 262176 | tf_op jit(solution)/shard_map/all_to_all | solution.py:18
  148.8 0.0 copy-start.3
  148.8 0.0 copy-start.4
  148.9 0.6 convert_element_type.188
  149.5 23.7 %all-to-all-start.7 = ((bf16[32,4,256]{2,1,0:T(4,128)(2,1)}), bf16[32,4,256]{2,1,0:T(4,128)(2,1)S(1)}, u32[]{:S(2)}, u32[]{:S(2)}) async-start(bf16[32,4,256]{2,1,0:T(4,128)(2,1)} %convert_element_type.188), calls=%async_computation.7 | async-start | bytes 131072 | tf_op jit(solution)/shard_map/all_to_all | solution.py:18
  173.2 1.1 convolution_convert_fusion.3
  174.3 0.0 copy-done.3
  174.3 1.2 convolution_convert_fusion.1
  175.5 9.2 %all-to-all-done.7 = bf16[32,4,256]{2,1,0:T(4,128)(2,1)S(1)} async-done(((bf16[32,4,256]{2,1,0:T(4,128)(2,1)}), bf16[32,4,256]{2,1,0:T(4,128)(2,1)S(1)}, u32[]{:S(2)}, u32[]{:S(2)}) %all-to-all-start.7) | async-done | bytes 65568 | tf_op jit(solution)/shard_map/all_to_all | solution.py:18
  184.8 0.6 add_convert_fusion.5
  (19 shorter events, 0.4 us)
Async XLA Ops:
  2.1 52.6 %all-to-all-start = ((bf16[32,16,128]{2,1,0:T(8,128)(2,1)}), bf16[32,16,128]{2,1,0:T(8,128)(2,1)S(1)}, u32[]{:S(2)}, u32[]{:S(2)}) async-start(bf16[32,16,128]{2,1,0:T(8,128)(2,1)} %bitcast.2), calls=%async_computation | async-start | bytes 262144 | tf_op jit(solution)/shard_map/all_to_all | solution.py:18
  33.2 7.8 %copy-start = (bf16[1024,172]{0,1:T(8,128)(2,1)S(1)}, bf16[1024,172]{0,1:T(8,128)(2,1)}, u32[]{:S(2)}) copy-start(bf16[1024,172]{0,1:T(8,128)(2,1)} %param.12) | copy-start | bytes 1056772
  33.2 7.8 %copy-start.1 = (bf16[1024,172]{0,1:T(8,128)(2,1)S(1)}, bf16[1024,172]{0,1:T(8,128)(2,1)}, u32[]{:S(2)}) copy-start(bf16[1024,172]{0,1:T(8,128)(2,1)} %param.11) | copy-start | bytes 1056772
  35.2 3.3 %collective-permute-start = (f32[176,256]{1,0:T(8,128)S(1)}, f32[176,256]{1,0:T(8,128)S(1)}, u32[]{:S(2)}, u32[]{:S(2)}) collective-permute-start(f32[176,256]{1,0:T(8,128)S(1)} %constant_dynamic-slice_fusion.1), channel_id=1, source_target_pairs={{0,128},{128,0},{1,129},{129,1},{2,130},{130,2},{3,131},{131,3},{4... | collective-permute-start | bytes 540680 | tf_op jit(solution)/shard_map/ppermute | solution.py:93
  38.5 11.9 %copy-start.2 = (s32[512]{0:T(512)S(1)}, s32[512]{0:T(512)}, u32[]{:S(2)}) copy-start(s32[512]{0:T(512)} %param.8) | copy-start | bytes 6148
  38.5 8.5 %collective-permute-start.1 = (f32[176,256]{1,0:T(8,128)S(1)}, f32[176,256]{1,0:T(8,128)S(1)}, u32[]{:S(2)}, u32[]{:S(2)}) collective-permute-start(f32[176,256]{1,0:T(8,128)S(1)} %dynamic-slice_add_fusion), channel_id=1, source_target_pairs={{0,256},{256,0},{512,768},{768,512},{1,257},{257,1},{513,769},{769... | collective-permute-start | bytes 540680 | tf_op jit(solution)/shard_map/ppermute | solution.py:97
  47.0 7.7 %collective-permute-start.2 = (f32[176,256]{1,0:T(8,128)S(1)}, f32[176,256]{1,0:T(8,128)S(1)}, u32[]{:S(2)}, u32[]{:S(2)}) collective-permute-start(f32[176,256]{1,0:T(8,128)S(1)} %add.140), channel_id=1, source_target_pairs={{0,768},{768,0},{256,512},{512,256},{1,769},{769,1},{257,513},{513... | collective-permute-start | bytes 540680 | tf_op jit(solution)/shard_map/ppermute | solution.py:98
  96.1 3.6 %collective-permute-start.3 = (f32[352,256]{1,0:T(8,128)S(1)}, f32[352,256]{1,0:T(8,128)S(1)}, u32[]{:S(2)}, u32[]{:S(2)}) collective-permute-start(f32[352,256]{1,0:T(8,128)S(1)} %constant_dynamic-slice_fusion), channel_id=1, source_target_pairs={{0,128},{128,0},{1,129},{129,1},{2,130},{130,2},{3,131},{131,3},{4... | collective-permute-start | bytes 1081352 | tf_op jit(solution)/shard_map/ppermute | solution.py:93
  138.1 10.7 %all-to-all-start.6 = ((bf16[4,128,256]{2,1,0:T(8,128)(2,1)}), bf16[4,128,256]{2,1,0:T(8,128)(2,1)S(1)}, u32[]{:S(2)}, u32[]{:S(2)}) async-start(bf16[4,128,256]{2,1,0:T(8,128)(2,1)} %pad_maximum_fusion.1), calls=%async_computation.6 | async-start | bytes 524288 | tf_op jit(solution)/shard_map/all_to_all | solution.py:18
  148.8 25.5 %copy-start.3 = (bf16[512,1024]{1,0:T(8,128)(2,1)S(1)}, bf16[512,1024]{1,0:T(8,128)(2,1)}, u32[]{:S(2)}) copy-start(bf16[512,1024]{1,0:T(8,128)(2,1)} %param.10) | copy-start | bytes 3145732
  148.8 25.5 %copy-start.4 = (f32[512]{0:T(512)S(1)}, f32[512]{0:T(512)}, u32[]{:S(2)}) copy-start(f32[512]{0:T(512)} %param.9) | copy-start | bytes 6148
  149.5 35.2 %all-to-all-start.7 = ((bf16[32,4,256]{2,1,0:T(4,128)(2,1)}), bf16[32,4,256]{2,1,0:T(4,128)(2,1)S(1)}, u32[]{:S(2)}, u32[]{:S(2)}) async-start(bf16[32,4,256]{2,1,0:T(4,128)(2,1)} %convert_element_type.188), calls=%async_computation.7 | async-start | bytes 131072 | tf_op jit(solution)/shard_map/all_to_all | solution.py:18

commit v6 on v5

--- a/solution.py
+++ b/solution.py
@@ -22,17 +22,13 @@
     return exchange(jnp.broadcast_to(x[None], (count,) + x.shape), axis, groups)
 
 
-def near(nz, count):
-    order = [(i + count // 2) % count for i in range(count)]
+def near(nz, count, turn):
+    order = [(i + turn) % count for i in range(count)]
     return [[i + j for j in order] for i in range(0, nz, count)]
 
 
-def ring_start(nz, count):
-    return 5 * nz // 8 // count * count + count // 2
-
-
-def ring(nz, count):
-    return [[(i + ring_start(nz, count)) % nz for i in range(nz)]]
+def ring(nz, turn):
+    return [[(i + turn) % nz for i in range(nz)]]
 
 
 def cut_lanes(x, count):
@@ -58,22 +54,22 @@
     here, width = tokens.shape
     cut = cut_lanes(tokens, PARTS)
     cut = jnp.broadcast_to(cut[None], (nz // PARTS,) + cut.shape).reshape(nz, here, width // PARTS)
-    return exchange(cut, "z", ring(nz, PARTS)).reshape(nz * here, width // PARTS)
+    return exchange(cut, "z", ring(nz, 5 * nz // 8)).reshape(nz * here, width // PARTS)
 
 
-def gather_routed(held, route_index):
+def share_slots(held, route_index):
     ny, nz = lax.axis_size("y"), lax.axis_size("z")
     count, part = held.shape
     rows = route_index.shape[0]
     place = route_index - lax.axis_index("y") * count
-    first = ring_start(nz, PARTS) * (count // nz)
+    turn = 5 * nz // 8
+    first = turn * (count // nz)
     held_at = jnp.where(place < first, place + (count - first), place - first)
     place = jnp.where((place >= 0) & (place < count), held_at, -1)
     pick = (place[:, None] == lax.broadcasted_iota(jnp.int32, (rows, count), 1)).astype(BF)
     filled = jnp.dot(pick, held, preferred_element_type=F32).astype(BF)
     got = add_up(exchange(filled.reshape(ny, rows // ny, part), "y")).astype(BF)
-    got = join_lanes(to_all(got, "z", PARTS, near(nz, PARTS)))
-    return to_all(got, "y", ny).reshape(rows, PARTS * part)
+    return to_all(got, "z", PARTS, near(nz, PARTS, turn % PARTS))
 
 
 def activate(gate, up, back):
@@ -93,9 +89,10 @@
     return keep + lax.ppermute(give, "core", [(0, 1), (1, 0)])
 
 
-def sum_by_pairs(part):
-    part = part + lax.ppermute(part, "x", [(0, 1), (1, 0), (2, 3), (3, 2)])
-    return part + lax.ppermute(part, "x", [(0, 3), (3, 0), (1, 2), (2, 1)])
+def add_neighbour(part, turn):
+    nx = lax.axis_size("x")
+    pairs = [((i + turn) % nx, ((i ^ 1) + turn) % nx) for i in range(nx)]
+    return part + lax.ppermute(part, "x", pairs)
 
 
 def scatter_rows(total, out_grad):
@@ -105,10 +102,11 @@
     each = slots // nz
     part = add_up(exchange(total.reshape(ny, slots, width), "y")).astype(BF)
     part = jnp.stack([part[:, i * quarter : (i + 1) * quarter] for i in range(NEAR)])
-    part = exchange(part, "z", near(nz, NEAR))
-    turn = ring_start(nz, NEAR) * each
-    part = jnp.concatenate([add_up(part[:, turn:]), add_up(part[:, :turn])]).astype(BF)
-    part = exchange(part.reshape(nz, each, quarter), "z", ring(nz, NEAR))
+    part = exchange(part, "z", near(nz, NEAR, 0))
+    turn = nz // 2
+    first = turn * each
+    part = jnp.concatenate([add_up(part[:, first:]), add_up(part[:, :first])]).astype(BF)
+    part = exchange(part.reshape(nz, each, quarter), "z", ring(nz, turn))
     part = add_up(part.reshape(nz // NEAR, NEAR, each, quarter)).transpose(1, 0, 2).reshape(each, width)
     first = lax.axis_index(("y", "z")) * each
     mine = lax.dynamic_slice_in_dim(out_grad, first, each, 0)
@@ -122,9 +120,13 @@
     both = jnp.concatenate([jnp.pad(gate_weight.T, more), jnp.pad(up_weight.T, more)])
     held = all_tokens_of_y(tokens)
     scaled = (router_score[:, None] * out_grad.astype(F32)).astype(BF)
-    back = sum_by_pairs(chip_sum(dot(jnp.pad(down_weight, more), scaled, 1, 1)))
+    back = add_neighbour(chip_sum(dot(jnp.pad(down_weight, more), scaled, 1, 1)), 0)
     held, back, both = lax.optimization_barrier((held, back, both))
-    routed = gather_routed(held, route_index)
+    slots = share_slots(held, route_index)
+    back = add_neighbour(back, 1)
+    slots, back = lax.optimization_barrier((slots, back))
+    ny = lax.axis_size("y")
+    routed = to_all(join_lanes(slots), "y", ny).reshape(route_index.shape[0], -1)
     sums = add_up(to_all(chip_sum(dot(both, routed, 1, 1)).astype(BF), "x", lax.axis_size("x")))
     grads = jnp.stack(activate(sums[:padded], sums[padded:], back))
     grads = lax.all_gather(grads, "core", axis=2, tiled=True)

time: 186 us -> 180 us (0.968)
  the two profiles are of different devices: /device:TPU:2 before, /device:TPU:1 now
where the time goes in v6:
time: 180 us; the launch traced here: 179 us
  starting transfers between devices  88.5 us (49%)
  blocking collectives  56.8 us (32%)
  waiting for transfers between devices  20.8 us (12%)
  matrix products  6.97 us (4%)
  local copies, waits for them, and re-layouts  3.35 us (2%)
  other arithmetic  2.07 us (1%)
    all_to_all x4, starting transfers between devices, exchange(): return lax.all_to_all(x, axis, 0, 0, tiled=True, axis_index_groups=groups)  70.3 us
    all_to_all x4, blocking collectives, exchange(): return lax.all_to_all(x, axis, 0, 0, tiled=True, axis_index_groups=groups)  53.5 us
    all_to_all x4, waiting for transfers between devices, exchange(): return lax.all_to_all(x, axis, 0, 0, tiled=True, axis_index_groups=groups)  10.8 us
    ppermute x2, starting transfers between devices, chip_sum(): return keep + lax.ppermute(give, 'core', [(0, 1), (1, 0)])  10.7 us
    ppermute x2, waiting for transfers between devices, add_neighbour(): return part + lax.ppermute(part, 'x', pairs)  7.86 us
    ppermute x2, starting transfers between devices, add_neighbour(): return part + lax.ppermute(part, 'x', pairs)  7.5 us
    dot_general x6, matrix products, dot(): lax.dot_general(a, b, (((i,), (j,)), ((), ())), preferred_element_type=F32)  6.61 us
  transfers between devices with their start and end apart: 8, of which 7 were waited for; matrix products, arithmetic and copies ran while one was open for 3% of the time, Pallas kernels for 0%

profile of v6, /device:TPU:1, one launch (start us, length us, event | category | flops | bytes accessed | tf_op | source)
XLA Modules:
  0.0 179.4 jit_solution(2581651570063564272)
XLA Ops:
  0.6 0.8 copy.25
  1.4 0.7 broadcast_in_dim.35
  2.1 31.3 %all-to-all-start = ((bf16[32,16,128]{2,1,0:T(8,128)(2,1)}), bf16[32,16,128]{2,1,0:T(8,128)(2,1)S(1)}, u32[]{:S(2)}, u32[]{:S(2)}) async-start(bf16[32,16,128]{2,1,0:T(8,128)(2,1)} %bitcast.2), calls=%async_computation | async-start | bytes 262144 | tf_op jit(solution)/shard_map/all_to_all | solution.py:18
  33.4 0.0 copy-start
  33.5 0.0 copy-start.1
  33.5 1.9 %fusion.4 = f32[176,512]{1,0:T(8,128)S(1)} fusion(bf16[512,1024]{1,0:T(8,128)(2,1)} %param.10, f32[512]{0:T(512)} %param.9, bf16[172,1024]{1,0:T(8,128)(2,1)} %param.13), kind=kOutput, calls=%fused_computation.14 | convolution fusion | flops 186122240 | bytes 1763328 | tf_op jit(solution)/shard_map/dot_general | solution.py:14
  35.4 0.0 copy-start.2
  35.4 3.1 %collective-permute-start = (f32[176,256]{1,0:T(8,128)S(1)}, f32[176,256]{1,0:T(8,128)S(1)}, u32[]{:S(2)}, u32[]{:S(2)}) collective-permute-start(f32[176,256]{1,0:T(8,128)S(1)} %constant_dynamic-slice_fusion.1), channel_id=1, source_target_pairs={{0,128},{128,0},{1,129},{129,1},{2,130},{130,2},{3,131},{131,3},{4... | collective-permute-start | bytes 540680 | tf_op jit(solution)/shard_map/ppermute | solution.py:89
  38.6 0.0 copy-done
  38.6 0.0 copy-done.1
  38.6 0.1 fusion.2
  38.7 0.9 collective-permute-done
  39.6 3.1 %collective-permute-start.1 = (f32[176,256]{1,0:T(8,128)S(1)}, f32[176,256]{1,0:T(8,128)S(1)}, u32[]{:S(2)}, u32[]{:S(2)}) collective-permute-start(f32[176,256]{1,0:T(8,128)S(1)} %dynamic-slice_add_fusion), channel_id=1, source_target_pairs={{0,256},{256,0},{512,768},{768,512},{1,257},{257,1},{513,769},{769... | collective-permute-start | bytes 540680 | tf_op jit(solution)/shard_map/ppermute | solution.py:95
  42.8 4.5 %collective-permute-done.1 = f32[176,256]{1,0:T(8,128)S(1)} collective-permute-done((f32[176,256]{1,0:T(8,128)S(1)}, f32[176,256]{1,0:T(8,128)S(1)}, u32[]{:S(2)}, u32[]{:S(2)}) %collective-permute-start.1) | collective-permute-done | bytes 180256 | tf_op jit(solution)/shard_map/ppermute | solution.py:95
  47.3 0.8 all-to-all-done
  48.2 0.4 convolution_convert_fusion.4
  48.5 8.8 %all_to_all.40 = bf16[4,128,128]{2,1,0:T(8,128)(2,1)S(1)} all-to-all(bf16[4,128,128]{2,1,0:T(8,128)(2,1)S(1)} %bitcast.103), channel_id=1, replica_groups=mesh['x'=4,'core'=2,'y'=4,'z'=32] {'y'}, dimensions={0} | all-to-all | bytes 262144 | tf_op jit(solution)/shard_map/all_to_all | solution.py:18
  57.4 0.7 broadcast_in_dim.38
  58.1 7.6 %all-to-all-start.2 = ((bf16[8,128,128]{2,1,0:T(8,128)(2,1)}), bf16[8,128,128]{2,1,0:T(8,128)(2,1)S(1)}, u32[]{:S(2)}, u32[]{:S(2)}) async-start(bf16[8,128,128]{2,1,0:T(8,128)(2,1)} %broadcast_in_dim.38), calls=%async_computation.2 | async-start | bytes 524288 | tf_op jit(solution)/shard_map/all_to_all | solution.py:18
  65.7 4.4 %collective-permute-start.2 = (f32[176,256]{1,0:T(8,128)S(1)}, f32[176,256]{1,0:T(8,128)S(1)}, u32[]{:S(2)}, u32[]{:S(2)}) collective-permute-start(f32[176,256]{1,0:T(8,128)S(1)} %add.140), channel_id=1, source_target_pairs={{256,512},{512,256},{768,0},{0,768},{257,513},{513,257},{769,1},{1... | collective-permute-start | bytes 540680 | tf_op jit(solution)/shard_map/ppermute | solution.py:95
  70.1 3.3 %collective-permute-done.2 = f32[176,256]{1,0:T(8,128)S(1)} collective-permute-done((f32[176,256]{1,0:T(8,128)S(1)}, f32[176,256]{1,0:T(8,128)S(1)}, u32[]{:S(2)}, u32[]{:S(2)}) %collective-permute-start.2) | collective-permute-done | bytes 180256 | tf_op jit(solution)/shard_map/ppermute | solution.py:95
  73.5 0.0 all-to-all-done.2
  73.5 0.2 copy.24
  73.7 0.1 broadcast_in_dim.40
  73.8 12.8 %all_to_all.41 = bf16[4,128,1024]{2,1,0:T(8,128)(2,1)S(1)} all-to-all(bf16[4,128,1024]{2,1,0:T(8,128)(2,1)S(1)} %broadcast_in_dim.40), channel_id=1, replica_groups=mesh['x'=4,'core'=2,'y'=4,'z'=32] {'y'}, dimensions={0} | all-to-all | bytes 2097152 | tf_op jit(solution)/shard_map/all_to_all | solution.py:18
  86.7 0.6 fusion.15
  87.3 7.5 %collective-permute-start.3 = (f32[352,256]{1,0:T(8,128)S(1)}, f32[352,256]{1,0:T(8,128)S(1)}, u32[]{:S(2)}, u32[]{:S(2)}) collective-permute-start(f32[352,256]{1,0:T(8,128)S(1)} %constant_dynamic-slice_fusion), channel_id=1, source_target_pairs={{0,128},{128,0},{1,129},{129,1},{2,130},{130,2},{3,131},{131,3},{4... | collective-permute-start | bytes 1081352 | tf_op jit(solution)/shard_map/ppermute | solution.py:89
  94.9 1.3 collective-permute-done.3
  96.1 0.1 add_convert_fusion.1
  96.3 14.6 %all_to_all.42 = bf16[4,352,256]{2,1,0:T(8,128)(2,1)S(1)} all-to-all(bf16[4,352,256]{2,1,0:T(8,128)(2,1)S(1)} %broadcast_in_dim.41), channel_id=1, replica_groups=mesh['x'=4,'core'=2,'y'=4,'z'=32] {'x'}, dimensions={0} | all-to-all | bytes 1441792 | tf_op jit(solution)/shard_map/all_to_all | solution.py:18
  110.9 0.1 convert_add_fusion
  110.9 0.1 fusion.10
  111.1 3.3 %all_gather.3 = bf16[3,176,512]{2,1,0:T(8,128)(2,1)S(1)} all-gather(bf16[3,176,256]{2,1,0:T(8,128)(2,1)S(1)} %pad_maximum_fusion), channel_id=1, replica_groups=mesh['x'=4,'core'=2,'y'=4,'z'=32] {'core'}, dimensions={2}, use_global_device_ids=true | all-gather | bytes 811008 | tf_op jit(solution)/shard_map/all_gather | solution.py:132
  114.5 0.7 convolution_convert_fusion
  115.2 17.3 %all_to_all.43 = bf16[4,128,1024]{2,1,0:T(8,128)(2,1)S(1)} all-to-all(bf16[4,128,1024]{2,1,0:T(8,128)(2,1)S(1)} %bitcast.94), channel_id=1, replica_groups=mesh['x'=4,'core'=2,'y'=4,'z'=32] {'y'}, dimensions={0} | all-to-all | bytes 2097152 | tf_op jit(solution)/shard_map/all_to_all | solution.py:18
  132.5 0.2 fusion.6
  132.7 0.7 pad_maximum_fusion.1
  133.4 3.4 %all-to-all-start.6 = ((bf16[4,128,256]{2,1,0:T(8,128)(2,1)}), bf16[4,128,256]{2,1,0:T(8,128)(2,1)S(1)}, u32[]{:S(2)}, u32[]{:S(2)}) async-start(bf16[4,128,256]{2,1,0:T(8,128)(2,1)} %pad_maximum_fusion.1), calls=%async_computation.6 | async-start | bytes 524288 | tf_op jit(solution)/shard_map/all_to_all | solution.py:18
  136.8 1.1 convolution_convert_fusion.2
  137.9 6.4 %all-to-all-done.6 = bf16[4,128,256]{2,1,0:T(8,128)(2,1)S(1)} async-done(((bf16[4,128,256]{2,1,0:T(8,128)(2,1)}), bf16[4,128,256]{2,1,0:T(8,128)(2,1)S(1)}, u32[]{:S(2)}, u32[]{:S(2)}) %all-to-all-start.6) | async-done | bytes 262176 | tf_op jit(solution)/shard_map/all_to_all | solution.py:18
  144.4 0.0 copy-start.3
  144.4 0.0 copy-start.4
  144.4 0.6 convert_element_type.188
  145.1 27.9 %all-to-all-start.7 = ((bf16[32,4,256]{2,1,0:T(4,128)(2,1)}), bf16[32,4,256]{2,1,0:T(4,128)(2,1)S(1)}, u32[]{:S(2)}, u32[]{:S(2)}) async-start(bf16[32,4,256]{2,1,0:T(4,128)(2,1)} %convert_element_type.188), calls=%async_computation.7 | async-start | bytes 131072 | tf_op jit(solution)/shard_map/all_to_all | solution.py:18
  173.0 1.1 convolution_convert_fusion.3
  174.1 1.2 convolution_convert_fusion.1
  175.3 3.5 %all-to-all-done.7 = bf16[32,4,256]{2,1,0:T(4,128)(2,1)S(1)} async-done(((bf16[32,4,256]{2,1,0:T(4,128)(2,1)}), bf16[32,4,256]{2,1,0:T(4,128)(2,1)S(1)}, u32[]{:S(2)}, u32[]{:S(2)}) %all-to-all-start.7) | async-done | bytes 65568 | tf_op jit(solution)/shard_map/all_to_all | solution.py:18
  178.8 0.6 add_convert_fusion.5
  (19 shorter events, 0.4 us)
Async XLA Ops:
  2.1 46.1 %all-to-all-start = ((bf16[32,16,128]{2,1,0:T(8,128)(2,1)}), bf16[32,16,128]{2,1,0:T(8,128)(2,1)S(1)}, u32[]{:S(2)}, u32[]{:S(2)}) async-start(bf16[32,16,128]{2,1,0:T(8,128)(2,1)} %bitcast.2), calls=%async_computation | async-start | bytes 262144 | tf_op jit(solution)/shard_map/all_to_all | solution.py:18
  33.4 5.2 %copy-start = (bf16[1024,172]{0,1:T(8,128)(2,1)S(1)}, bf16[1024,172]{0,1:T(8,128)(2,1)}, u32[]{:S(2)}) copy-start(bf16[1024,172]{0,1:T(8,128)(2,1)} %param.12) | copy-start | bytes 1056772
  33.5 5.2 %copy-start.1 = (bf16[1024,172]{0,1:T(8,128)(2,1)S(1)}, bf16[1024,172]{0,1:T(8,128)(2,1)}, u32[]{:S(2)}) copy-start(bf16[1024,172]{0,1:T(8,128)(2,1)} %param.11) | copy-start | bytes 1056772
  35.4 7.3 %copy-start.2 = (s32[512]{0:T(512)S(1)}, s32[512]{0:T(512)}, u32[]{:S(2)}) copy-start(s32[512]{0:T(512)} %param.8) | copy-start | bytes 6148
  35.4 4.2 %collective-permute-start = (f32[176,256]{1,0:T(8,128)S(1)}, f32[176,256]{1,0:T(8,128)S(1)}, u32[]{:S(2)}, u32[]{:S(2)}) collective-permute-start(f32[176,256]{1,0:T(8,128)S(1)} %constant_dynamic-slice_fusion.1), channel_id=1, source_target_pairs={{0,128},{128,0},{1,129},{129,1},{2,130},{130,2},{3,131},{131,3},{4... | collective-permute-start | bytes 540680 | tf_op jit(solution)/shard_map/ppermute | solution.py:89
  39.6 7.7 %collective-permute-start.1 = (f32[176,256]{1,0:T(8,128)S(1)}, f32[176,256]{1,0:T(8,128)S(1)}, u32[]{:S(2)}, u32[]{:S(2)}) collective-permute-start(f32[176,256]{1,0:T(8,128)S(1)} %dynamic-slice_add_fusion), channel_id=1, source_target_pairs={{0,256},{256,0},{512,768},{768,512},{1,257},{257,1},{513,769},{769... | collective-permute-start | bytes 540680 | tf_op jit(solution)/shard_map/ppermute | solution.py:95
  58.1 15.4 %all-to-all-start.2 = ((bf16[8,128,128]{2,1,0:T(8,128)(2,1)}), bf16[8,128,128]{2,1,0:T(8,128)(2,1)S(1)}, u32[]{:S(2)}, u32[]{:S(2)}) async-start(bf16[8,128,128]{2,1,0:T(8,128)(2,1)} %broadcast_in_dim.38), calls=%async_computation.2 | async-start | bytes 524288 | tf_op jit(solution)/shard_map/all_to_all | solution.py:18
  65.7 7.7 %collective-permute-start.2 = (f32[176,256]{1,0:T(8,128)S(1)}, f32[176,256]{1,0:T(8,128)S(1)}, u32[]{:S(2)}, u32[]{:S(2)}) collective-permute-start(f32[176,256]{1,0:T(8,128)S(1)} %add.140), channel_id=1, source_target_pairs={{256,512},{512,256},{768,0},{0,768},{257,513},{513,257},{769,1},{1... | collective-permute-start | bytes 540680 | tf_op jit(solution)/shard_map/ppermute | solution.py:95
  87.3 8.8 %collective-permute-start.3 = (f32[352,256]{1,0:T(8,128)S(1)}, f32[352,256]{1,0:T(8,128)S(1)}, u32[]{:S(2)}, u32[]{:S(2)}) collective-permute-start(f32[352,256]{1,0:T(8,128)S(1)} %constant_dynamic-slice_fusion), channel_id=1, source_target_pairs={{0,128},{128,0},{1,129},{129,1},{2,130},{130,2},{3,131},{131,3},{4... | collective-permute-start | bytes 1081352 | tf_op jit(solution)/shard_map/ppermute | solution.py:89
  133.4 11.0 %all-to-all-start.6 = ((bf16[4,128,256]{2,1,0:T(8,128)(2,1)}), bf16[4,128,256]{2,1,0:T(8,128)(2,1)S(1)}, u32[]{:S(2)}, u32[]{:S(2)}) async-start(bf16[4,128,256]{2,1,0:T(8,128)(2,1)} %pad_maximum_fusion.1), calls=%async_computation.6 | async-start | bytes 524288 | tf_op jit(solution)/shard_map/all_to_all | solution.py:18
  144.4 29.7 %copy-start.3 = (bf16[512,1024]{1,0:T(8,128)(2,1)S(1)}, bf16[512,1024]{1,0:T(8,128)(2,1)}, u32[]{:S(2)}) copy-start(bf16[512,1024]{1,0:T(8,128)(2,1)} %param.10) | copy-start | bytes 3145732
  144.4 29.7 %copy-start.4 = (f32[512]{0:T(512)S(1)}, f32[512]{0:T(512)}, u32[]{:S(2)}) copy-start(f32[512]{0:T(512)} %param.9) | copy-start | bytes 6148
  145.1 33.7 %all-to-all-start.7 = ((bf16[32,4,256]{2,1,0:T(4,128)(2,1)}), bf16[32,4,256]{2,1,0:T(4,128)(2,1)S(1)}, u32[]{:S(2)}, u32[]{:S(2)}) async-start(bf16[32,4,256]{2,1,0:T(4,128)(2,1)} %convert_element_type.188), calls=%async_computation.7 | async-start | bytes 131072 | tf_op jit(solution)/shard_map/all_to_all | solution.py:18

commit v7 on v6

--- a/solution.py
+++ b/solution.py
@@ -103,7 +103,7 @@
     part = add_up(exchange(total.reshape(ny, slots, width), "y")).astype(BF)
     part = jnp.stack([part[:, i * quarter : (i + 1) * quarter] for i in range(NEAR)])
     part = exchange(part, "z", near(nz, NEAR, 0))
-    turn = nz // 2
+    turn = 3 * nz // 4
     first = turn * each
     part = jnp.concatenate([add_up(part[:, first:]), add_up(part[:, :first])]).astype(BF)
     part = exchange(part.reshape(nz, each, quarter), "z", ring(nz, turn))

time: 180 us -> 182 us (1.011)
  the two profiles are of different devices: /device:TPU:1 before, /device:TPU:2 now
where the time goes in v7:
time: 182 us; the launch traced here: 181 us
  starting transfers between devices  72.1 us (40%)
  blocking collectives  59.1 us (32%)
  waiting for transfers between devices  36.4 us (20%)
  matrix products  6.96 us (4%)
  local copies, waits for them, and re-layouts  3.36 us (2%)
  other arithmetic  2.06 us (1%)
    all_to_all x4, starting transfers between devices, exchange(): return lax.all_to_all(x, axis, 0, 0, tiled=True, axis_index_groups=groups)  62.4 us
    all_to_all x4, blocking collectives, exchange(): return lax.all_to_all(x, axis, 0, 0, tiled=True, axis_index_groups=groups)  56.9 us
    all_to_all x4, waiting for transfers between devices, exchange(): return lax.all_to_all(x, axis, 0, 0, tiled=True, axis_index_groups=groups)  23.4 us
    ppermute x2, waiting for transfers between devices, add_neighbour(): return part + lax.ppermute(part, 'x', pairs)  10 us
    dot_general x6, matrix products, dot(): lax.dot_general(a, b, (((i,), (j,)), ((), ())), preferred_element_type=F32)  6.6 us
    ppermute x2, starting transfers between devices, add_neighbour(): return part + lax.ppermute(part, 'x', pairs)  5.83 us
    ppermute x2, starting transfers between devices, chip_sum(): return keep + lax.ppermute(give, 'core', [(0, 1), (1, 0)])  3.84 us
  transfers between devices with their start and end apart: 8, of which 8 were waited for; matrix products, arithmetic and copies ran while one was open for 3% of the time, Pallas kernels for 0%

profile of v7, /device:TPU:2, one launch (start us, length us, event | category | flops | bytes accessed | tf_op | source)
XLA Modules:
  0.0 180.8 jit_solution(9225212643153175424)
XLA Ops:
  0.6 0.8 copy.25
  1.4 0.7 broadcast_in_dim.35
  2.1 31.1 %all-to-all-start = ((bf16[32,16,128]{2,1,0:T(8,128)(2,1)}), bf16[32,16,128]{2,1,0:T(8,128)(2,1)S(1)}, u32[]{:S(2)}, u32[]{:S(2)}) async-start(bf16[32,16,128]{2,1,0:T(8,128)(2,1)} %bitcast.2), calls=%async_computation | async-start | bytes 262144 | tf_op jit(solution)/shard_map/all_to_all | solution.py:18
  33.2 0.0 copy-start
  33.2 0.0 copy-start.1
  33.2 1.9 %fusion.4 = f32[176,512]{1,0:T(8,128)S(1)} fusion(bf16[512,1024]{1,0:T(8,128)(2,1)} %param.10, f32[512]{0:T(512)} %param.9, bf16[172,1024]{1,0:T(8,128)(2,1)} %param.13), kind=kOutput, calls=%fused_computation.14 | convolution fusion | flops 186122240 | bytes 1763328 | tf_op jit(solution)/shard_map/dot_general | solution.py:14
  35.2 0.0 copy-start.2
  35.2 1.9 %collective-permute-start = (f32[176,256]{1,0:T(8,128)S(1)}, f32[176,256]{1,0:T(8,128)S(1)}, u32[]{:S(2)}, u32[]{:S(2)}) collective-permute-start(f32[176,256]{1,0:T(8,128)S(1)} %constant_dynamic-slice_fusion.1), channel_id=1, source_target_pairs={{0,128},{128,0},{1,129},{129,1},{2,130},{130,2},{3,131},{131,3},{4... | collective-permute-start | bytes 540680 | tf_op jit(solution)/shard_map/ppermute | solution.py:89
  37.1 0.0 copy-done
  37.1 0.1 fusion.2
  37.2 1.3 collective-permute-done
  38.5 2.4 %collective-permute-start.1 = (f32[176,256]{1,0:T(8,128)S(1)}, f32[176,256]{1,0:T(8,128)S(1)}, u32[]{:S(2)}, u32[]{:S(2)}) collective-permute-start(f32[176,256]{1,0:T(8,128)S(1)} %dynamic-slice_add_fusion), channel_id=1, source_target_pairs={{0,256},{256,0},{512,768},{768,512},{1,257},{257,1},{513,769},{769... | collective-permute-start | bytes 540680 | tf_op jit(solution)/shard_map/ppermute | solution.py:95
  41.0 0.0 copy-done.2
  41.0 6.0 %collective-permute-done.1 = f32[176,256]{1,0:T(8,128)S(1)} collective-permute-done((f32[176,256]{1,0:T(8,128)S(1)}, f32[176,256]{1,0:T(8,128)S(1)}, u32[]{:S(2)}, u32[]{:S(2)}) %collective-permute-start.1) | collective-permute-done | bytes 180256 | tf_op jit(solution)/shard_map/ppermute | solution.py:95
  47.0 2.4 %all-to-all-done = bf16[32,16,128]{2,1,0:T(8,128)(2,1)S(1)} async-done(((bf16[32,16,128]{2,1,0:T(8,128)(2,1)}), bf16[32,16,128]{2,1,0:T(8,128)(2,1)S(1)}, u32[]{:S(2)}, u32[]{:S(2)}) %all-to-all-start) | async-done | bytes 131104 | tf_op jit(solution)/shard_map/all_to_all | solution.py:18
  49.5 0.4 convolution_convert_fusion.4
  49.8 10.2 %all_to_all.40 = bf16[4,128,128]{2,1,0:T(8,128)(2,1)S(1)} all-to-all(bf16[4,128,128]{2,1,0:T(8,128)(2,1)S(1)} %bitcast.103), channel_id=1, replica_groups=mesh['x'=4,'core'=2,'y'=4,'z'=32] {'y'}, dimensions={0} | all-to-all | bytes 262144 | tf_op jit(solution)/shard_map/all_to_all | solution.py:18
  60.1 0.7 broadcast_in_dim.38
  60.8 7.2 %all-to-all-start.2 = ((bf16[8,128,128]{2,1,0:T(8,128)(2,1)}), bf16[8,128,128]{2,1,0:T(8,128)(2,1)S(1)}, u32[]{:S(2)}, u32[]{:S(2)}) async-start(bf16[8,128,128]{2,1,0:T(8,128)(2,1)} %broadcast_in_dim.38), calls=%async_computation.2 | async-start | bytes 524288 | tf_op jit(solution)/shard_map/all_to_all | solution.py:18
  68.1 3.4 %collective-permute-start.2 = (f32[176,256]{1,0:T(8,128)S(1)}, f32[176,256]{1,0:T(8,128)S(1)}, u32[]{:S(2)}, u32[]{:S(2)}) collective-permute-start(f32[176,256]{1,0:T(8,128)S(1)} %add.140), channel_id=1, source_target_pairs={{256,512},{512,256},{768,0},{0,768},{257,513},{513,257},{769,1},{1... | collective-permute-start | bytes 540680 | tf_op jit(solution)/shard_map/ppermute | solution.py:95
  71.4 4.0 %collective-permute-done.2 = f32[176,256]{1,0:T(8,128)S(1)} collective-permute-done((f32[176,256]{1,0:T(8,128)S(1)}, f32[176,256]{1,0:T(8,128)S(1)}, u32[]{:S(2)}, u32[]{:S(2)}) %collective-permute-start.2) | collective-permute-done | bytes 180256 | tf_op jit(solution)/shard_map/ppermute | solution.py:95
  75.5 1.2 all-to-all-done.2
  76.7 0.2 copy.24
  76.9 0.1 broadcast_in_dim.40
  77.1 13.3 %all_to_all.41 = bf16[4,128,1024]{2,1,0:T(8,128)(2,1)S(1)} all-to-all(bf16[4,128,1024]{2,1,0:T(8,128)(2,1)S(1)} %broadcast_in_dim.40), channel_id=1, replica_groups=mesh['x'=4,'core'=2,'y'=4,'z'=32] {'y'}, dimensions={0} | all-to-all | bytes 2097152 | tf_op jit(solution)/shard_map/all_to_all | solution.py:18
  90.4 0.6 fusion.15
  91.0 1.9 %collective-permute-start.3 = (f32[352,256]{1,0:T(8,128)S(1)}, f32[352,256]{1,0:T(8,128)S(1)}, u32[]{:S(2)}, u32[]{:S(2)}) collective-permute-start(f32[352,256]{1,0:T(8,128)S(1)} %constant_dynamic-slice_fusion), channel_id=1, source_target_pairs={{0,128},{128,0},{1,129},{129,1},{2,130},{130,2},{3,131},{131,3},{4... | collective-permute-start | bytes 1081352 | tf_op jit(solution)/shard_map/ppermute | solution.py:89
  92.9 1.6 collective-permute-done.3
  94.6 0.1 add_convert_fusion.1
  94.7 15.3 %all_to_all.42 = bf16[4,352,256]{2,1,0:T(8,128)(2,1)S(1)} all-to-all(bf16[4,352,256]{2,1,0:T(8,128)(2,1)S(1)} %broadcast_in_dim.41), channel_id=1, replica_groups=mesh['x'=4,'core'=2,'y'=4,'z'=32] {'x'}, dimensions={0} | all-to-all | bytes 1441792 | tf_op jit(solution)/shard_map/all_to_all | solution.py:18
  109.9 0.1 convert_add_fusion
  110.0 0.1 fusion.10
  110.2 2.2 %all_gather.3 = bf16[3,176,512]{2,1,0:T(8,128)(2,1)S(1)} all-gather(bf16[3,176,256]{2,1,0:T(8,128)(2,1)S(1)} %pad_maximum_fusion), channel_id=1, replica_groups=mesh['x'=4,'core'=2,'y'=4,'z'=32] {'core'}, dimensions={2}, use_global_device_ids=true | all-gather | bytes 811008 | tf_op jit(solution)/shard_map/all_gather | solution.py:132
  112.4 0.7 convolution_convert_fusion
  113.1 18.1 %all_to_all.43 = bf16[4,128,1024]{2,1,0:T(8,128)(2,1)S(1)} all-to-all(bf16[4,128,1024]{2,1,0:T(8,128)(2,1)S(1)} %bitcast.94), channel_id=1, replica_groups=mesh['x'=4,'core'=2,'y'=4,'z'=32] {'y'}, dimensions={0} | all-to-all | bytes 2097152 | tf_op jit(solution)/shard_map/all_to_all | solution.py:18
  131.2 0.2 fusion.6
  131.4 0.7 pad_maximum_fusion.1
  132.2 3.4 %all-to-all-start.6 = ((bf16[4,128,256]{2,1,0:T(8,128)(2,1)}), bf16[4,128,256]{2,1,0:T(8,128)(2,1)S(1)}, u32[]{:S(2)}, u32[]{:S(2)}) async-start(bf16[4,128,256]{2,1,0:T(8,128)(2,1)} %pad_maximum_fusion.1), calls=%async_computation.6 | async-start | bytes 524288 | tf_op jit(solution)/shard_map/all_to_all | solution.py:18
  135.6 1.1 convolution_convert_fusion.2
  136.7 7.5 %all-to-all-done.6 = bf16[4,128,256]{2,1,0:T(8,128)(2,1)S(1)} async-done(((bf16[4,128,256]{2,1,0:T(8,128)(2,1)}), bf16[4,128,256]{2,1,0:T(8,128)(2,1)S(1)}, u32[]{:S(2)}, u32[]{:S(2)}) %all-to-all-start.6) | async-done | bytes 262176 | tf_op jit(solution)/shard_map/all_to_all | solution.py:18
  144.2 0.0 copy-start.3
  144.2 0.0 copy-start.4
  144.3 0.7 convert_element_type.188
  144.9 20.7 %all-to-all-start.7 = ((bf16[32,4,256]{2,1,0:T(4,128)(2,1)}), bf16[32,4,256]{2,1,0:T(4,128)(2,1)S(1)}, u32[]{:S(2)}, u32[]{:S(2)}) async-start(bf16[32,4,256]{2,1,0:T(4,128)(2,1)} %convert_element_type.188), calls=%async_computation.7 | async-start | bytes 131072 | tf_op jit(solution)/shard_map/all_to_all | solution.py:18
  165.6 1.1 convolution_convert_fusion.3
  166.7 1.2 convolution_convert_fusion.1
  167.9 12.3 %all-to-all-done.7 = bf16[32,4,256]{2,1,0:T(4,128)(2,1)S(1)} async-done(((bf16[32,4,256]{2,1,0:T(4,128)(2,1)}), bf16[32,4,256]{2,1,0:T(4,128)(2,1)S(1)}, u32[]{:S(2)}, u32[]{:S(2)}) %all-to-all-start.7) | async-done | bytes 65568 | tf_op jit(solution)/shard_map/all_to_all | solution.py:18
  180.2 0.6 add_convert_fusion.5
  (20 shorter events, 0.4 us)
Async XLA Ops:
  2.1 47.4 %all-to-all-start = ((bf16[32,16,128]{2,1,0:T(8,128)(2,1)}), bf16[32,16,128]{2,1,0:T(8,128)(2,1)S(1)}, u32[]{:S(2)}, u32[]{:S(2)}) async-start(bf16[32,16,128]{2,1,0:T(8,128)(2,1)} %bitcast.2), calls=%async_computation | async-start | bytes 262144 | tf_op jit(solution)/shard_map/all_to_all | solution.py:18
  33.2 3.9 %copy-start = (bf16[1024,172]{0,1:T(8,128)(2,1)S(1)}, bf16[1024,172]{0,1:T(8,128)(2,1)}, u32[]{:S(2)}) copy-start(bf16[1024,172]{0,1:T(8,128)(2,1)} %param.12) | copy-start | bytes 1056772
  33.2 3.9 %copy-start.1 = (bf16[1024,172]{0,1:T(8,128)(2,1)S(1)}, bf16[1024,172]{0,1:T(8,128)(2,1)}, u32[]{:S(2)}) copy-start(bf16[1024,172]{0,1:T(8,128)(2,1)} %param.11) | copy-start | bytes 1056772
  35.2 5.8 %copy-start.2 = (s32[512]{0:T(512)S(1)}, s32[512]{0:T(512)}, u32[]{:S(2)}) copy-start(s32[512]{0:T(512)} %param.8) | copy-start | bytes 6148
  35.2 3.3 %collective-permute-start = (f32[176,256]{1,0:T(8,128)S(1)}, f32[176,256]{1,0:T(8,128)S(1)}, u32[]{:S(2)}, u32[]{:S(2)}) collective-permute-start(f32[176,256]{1,0:T(8,128)S(1)} %constant_dynamic-slice_fusion.1), channel_id=1, source_target_pairs={{0,128},{128,0},{1,129},{129,1},{2,130},{130,2},{3,131},{131,3},{4... | collective-permute-start | bytes 540680 | tf_op jit(solution)/shard_map/ppermute | solution.py:89
  38.5 8.5 %collective-permute-start.1 = (f32[176,256]{1,0:T(8,128)S(1)}, f32[176,256]{1,0:T(8,128)S(1)}, u32[]{:S(2)}, u32[]{:S(2)}) collective-permute-start(f32[176,256]{1,0:T(8,128)S(1)} %dynamic-slice_add_fusion), channel_id=1, source_target_pairs={{0,256},{256,0},{512,768},{768,512},{1,257},{257,1},{513,769},{769... | collective-permute-start | bytes 540680 | tf_op jit(solution)/shard_map/ppermute | solution.py:95
  60.8 15.8 %all-to-all-start.2 = ((bf16[8,128,128]{2,1,0:T(8,128)(2,1)}), bf16[8,128,128]{2,1,0:T(8,128)(2,1)S(1)}, u32[]{:S(2)}, u32[]{:S(2)}) async-start(bf16[8,128,128]{2,1,0:T(8,128)(2,1)} %broadcast_in_dim.38), calls=%async_computation.2 | async-start | bytes 524288 | tf_op jit(solution)/shard_map/all_to_all | solution.py:18
  68.1 7.4 %collective-permute-start.2 = (f32[176,256]{1,0:T(8,128)S(1)}, f32[176,256]{1,0:T(8,128)S(1)}, u32[]{:S(2)}, u32[]{:S(2)}) collective-permute-start(f32[176,256]{1,0:T(8,128)S(1)} %add.140), channel_id=1, source_target_pairs={{256,512},{512,256},{768,0},{0,768},{257,513},{513,257},{769,1},{1... | collective-permute-start | bytes 540680 | tf_op jit(solution)/shard_map/ppermute | solution.py:95
  91.0 3.6 %collective-permute-start.3 = (f32[352,256]{1,0:T(8,128)S(1)}, f32[352,256]{1,0:T(8,128)S(1)}, u32[]{:S(2)}, u32[]{:S(2)}) collective-permute-start(f32[352,256]{1,0:T(8,128)S(1)} %constant_dynamic-slice_fusion), channel_id=1, source_target_pairs={{0,128},{128,0},{1,129},{129,1},{2,130},{130,2},{3,131},{131,3},{4... | collective-permute-start | bytes 1081352 | tf_op jit(solution)/shard_map/ppermute | solution.py:89
  132.2 12.0 %all-to-all-start.6 = ((bf16[4,128,256]{2,1,0:T(8,128)(2,1)}), bf16[4,128,256]{2,1,0:T(8,128)(2,1)S(1)}, u32[]{:S(2)}, u32[]{:S(2)}) async-start(bf16[4,128,256]{2,1,0:T(8,128)(2,1)} %pad_maximum_fusion.1), calls=%async_computation.6 | async-start | bytes 524288 | tf_op jit(solution)/shard_map/all_to_all | solution.py:18
  144.2 22.5 %copy-start.3 = (bf16[512,1024]{1,0:T(8,128)(2,1)S(1)}, bf16[512,1024]{1,0:T(8,128)(2,1)}, u32[]{:S(2)}) copy-start(bf16[512,1024]{1,0:T(8,128)(2,1)} %param.10) | copy-start | bytes 3145732
  144.2 22.5 %copy-start.4 = (f32[512]{0:T(512)S(1)}, f32[512]{0:T(512)}, u32[]{:S(2)}) copy-start(f32[512]{0:T(512)} %param.9) | copy-start | bytes 6148
  144.9 35.3 %all-to-all-start.7 = ((bf16[32,4,256]{2,1,0:T(4,128)(2,1)}), bf16[32,4,256]{2,1,0:T(4,128)(2,1)S(1)}, u32[]{:S(2)}, u32[]{:S(2)}) async-start(bf16[32,4,256]{2,1,0:T(4,128)(2,1)} %convert_element_type.188), calls=%async_computation.7 | async-start | bytes 131072 | tf_op jit(solution)/shard_map/all_to_all | solution.py:18
